TPU v7x, 512 devices: a whole 4x4x16 slice. The times are simulated.
512 devices in a mesh: grp: 8 (over z_lo, core), slab: 64 (over y, z_hi, x).
Axes of the slice: x: 4, y: 4, z: 16 (z_hi: 4, z_lo: 4; z = z_hi * 4 + z_lo), core: 2. Of those that a mesh axis runs over, the one named last changes fastest.
Arguments:
- adjoint: float32 [9, 128, 128, 128], P(None, 'grp', 'slab'), may hold values from -6 to 6
- source: float32 [9, 128, 128, 128], P(None, 'grp', 'slab'), may hold values from -6 to 6
- contrast: float32 [7, 9, 9], replicated, may hold values from -2 to 2
- phase_id: int32 [128, 128, 128], P('grp', 'slab'), may hold values 0 or 1
- grain_id: int32 [128, 128, 128], P('grp', 'slab'), may hold values from 0 to 4095
- orientation: int32 [4096], replicated, may hold values from 0 to 5
Outputs:
- updated: float32 [9, 128, 128, 128], P(None, 'grp', 'slab')
Inputs may be any that keep to these rules, and one draw needn't show every extreme that they name: `phase_id`: 1 marks a ceramic voxel, 0 a polymer voxel.
All inputs are finite; a program needn't handle non-finite values. No bound on the sum of `phase_id` on one device may be relied on, other than what follows from the above.
Results may differ from a plain program's by a relative error of at most 0.0001.
Values sent between devices are 32-bit elements; how exact they have to be, the bound alone decides.
A program may use at most 64 MiB of HBM per device.

v0:
```python
import functools

import jax
import jax.numpy as jnp
import ml_dtypes
import numpy as np
from jax import lax
from jax.experimental import pallas as pl
from jax.experimental.pallas import tpu as pltpu
from jax.sharding import PartitionSpec as P

N = 128
GRP = 8
SLAB = 64
F32 = jnp.float32
BF16 = jnp.bfloat16
ROOT_HALF = float(np.sqrt(0.5))
MESH = pl.DeviceIdType.MESH


def split_const(matrix, axis):
    high = matrix.astype(ml_dtypes.bfloat16)
    low = (matrix - high.astype(np.float64)).astype(ml_dtypes.bfloat16)
    return np.concatenate([high, high, low], axis=axis)


def angle(a, b, length=N):
    return 2.0 * np.pi * ((np.asarray(a) * np.asarray(b)) % length) / length


def x_tables():
    x = np.arange(N)
    forward = np.zeros((SLAB, 2, N))
    inverse = np.zeros((SLAB, 2, N))
    for k in range(1, SLAB):
        forward[k, 0] = np.cos(angle(k, x))
        forward[k, 1] = -np.sin(angle(k, x))
    forward[0, 0] = 1.0
    forward[0, 1] = (-1.0) ** x
    inverse[1:] = 2.0 * forward[1:]
    inverse[0] = forward[0]
    return forward.reshape(N, N), inverse.reshape(N, N)


def z_tables(first):
    z = np.arange(N).reshape(SLAB, 2)
    forward = np.zeros((2, GRP, 2, 8, 2, SLAB, 2))
    inverse = np.zeros((2, SLAB, 2, 2, GRP, 2, 8))
    for m in range(SLAB):
        hi, lo = divmod(m, 8)
        for h in range(2):
            for z2 in range(2):
                if first:
                    cos, sin = np.cos(angle(m, z[:, z2])), np.sin(angle(m, z[:, z2]))
                    if m == 0:
                        alt = (-1.0) ** z[:, z2]
                        forward[h, hi, 0, lo, z2, :, h] = 1.0
                        forward[h, hi, 1, lo, z2, :, h] = alt
                        inverse[z2, :, h, h, hi, 0, lo] = 1.0
                        inverse[z2, :, h, h, hi, 1, lo] = alt
                    else:
                        forward[h, hi, 0, lo, z2, :, h] = cos
                        forward[h, hi, 1, lo, z2, :, h] = -sin
                        inverse[z2, :, h, h, hi, 0, lo] = 2.0 * cos
                        inverse[z2, :, h, h, hi, 1, lo] = -2.0 * sin
                else:
                    k = m if h == 0 else (64 if m == 0 else N - m)
                    cos, sin = np.cos(angle(k, z[:, z2])), np.sin(angle(k, z[:, z2]))
                    forward[h, hi, 0, lo, z2, :, 0] = cos
                    forward[h, hi, 0, lo, z2, :, 1] = sin
                    forward[h, hi, 1, lo, z2, :, 0] = -sin
                    forward[h, hi, 1, lo, z2, :, 1] = cos
                    inverse[z2, :, 0, h, hi, 0, lo] = cos
                    inverse[z2, :, 0, h, hi, 1, lo] = -sin
                    inverse[z2, :, 1, h, hi, 0, lo] = sin
                    inverse[z2, :, 1, h, hi, 1, lo] = cos
    return forward.reshape(256, 256), inverse.reshape(256, 256)


def y_outer_tables(corner):
    forward = np.zeros((2, 72, GRP, 2, 8))
    inverse = np.zeros((GRP, 2, 8, 2, 72))
    g = np.arange(GRP)
    for k1 in range(8):
        cos, sin = np.cos(angle(k1, g, 8)), np.sin(angle(k1, g, 8))
        for kz in range(8):
            row = k1 * 8 + kz
            if corner and kz == 0:
                for source, target in ((0, row), (1, 64 + k1)):
                    forward[0, target, :, source, kz] = cos
                    forward[1, target, :, source, kz] = -sin
                    inverse[:, source, kz, 0, target] = cos
                    inverse[:, source, kz, 1, target] = -sin
            else:
                forward[0, row, :, 0, kz] = cos
                forward[0, row, :, 1, kz] = sin
                forward[1, row, :, 0, kz] = -sin
                forward[1, row, :, 1, kz] = cos
                inverse[:, 0, kz, 0, row] = cos
                inverse[:, 0, kz, 1, row] = -sin
                inverse[:, 1, kz, 0, row] = sin
                inverse[:, 1, kz, 1, row] = cos
    return forward.reshape(144, 128), inverse.reshape(128, 144)


def lane_parts():
    lane = np.arange(N)
    return lane // 32, lane // 2 % 16, lane % 2


def y_inner_tables():
    c, y, h = lane_parts()
    same = (c[:, None] == c[None, :]) & (h[:, None] == h[None, :])
    cos = np.where(same, np.cos(angle(y[:, None], y[None, :], 16)), 0.0)
    sin = np.where(same, np.sin(angle(y[:, None], y[None, :], 16)), 0.0)
    forward = np.block([[cos, -sin], [sin, cos]])
    inverse = np.block([[cos, sin], [-sin, cos]])
    return forward, inverse


def row_k1():
    return np.concatenate([np.repeat(np.arange(8), 8), np.arange(8)])


def twiddle_tables():
    _, y, _ = lane_parts()
    turn = angle(row_k1()[:, None], y[None, :])
    return np.stack([np.cos(turn), np.sin(turn)]).astype(np.float32)


def symbol(k):
    turn = 2.0 * np.pi * (np.asarray(k) % N) / N
    return np.stack([np.cos(turn) - 1.0, np.sin(turn)]).astype(np.float32)


def symbol_tables():
    _, k2, h = lane_parts()
    along_y = symbol(row_k1()[:, None] + 8 * k2[None, :])
    along_x = np.zeros((SLAB, 2, 8, N), np.float32)
    for s in range(SLAB):
        k = np.where(h == 0, 0, 64) if s == 0 else np.full(N, s)
        along_x[s] = np.broadcast_to(symbol(k)[:, None, :], (2, 8, N))
    along_z = np.zeros((2 * GRP, 2, 16, N), np.float32)
    for first in range(2):
        for g in range(GRP):
            for row in range(16):
                m = g * 8 + row
                if row >= 8:
                    k = np.full(N, 64)
                elif first:
                    k = np.full(N, m)
                else:
                    k = np.where(h == 0, m, 64 if m == 0 else N - m)
                along_z[first * GRP + g, :, row] = symbol(k)
    return along_x, along_y, along_z


@functools.cache
def constants():
    x_forward, x_inverse = x_tables()
    z_pairs = [z_tables(first) for first in (False, True)]
    y_pairs = [y_outer_tables(corner) for corner in (False, True)]
    inner_forward, inner_inverse = y_inner_tables()
    along_x, along_y, along_z = symbol_tables()
    return dict(
        wx=split_const(x_forward, 1),
        wxi=split_const(x_inverse, 0),
        wz=np.stack([split_const(pair[0], 1) for pair in z_pairs]),
        wzi=np.stack([split_const(pair[1], 1) for pair in z_pairs]),
        wy=np.stack([split_const(pair[0], 1) for pair in y_pairs]),
        wyi=np.stack([split_const(pair[1], 1) for pair in y_pairs]),
        wl=split_const(inner_forward, 0),
        wli=split_const(inner_inverse, 0),
        tw=twiddle_tables(),
        dx=along_x,
        dy=along_y,
        dz=along_z,
    )


CONSTANTS = ("wx", "wxi", "wz", "wzi", "wy", "wyi", "wl", "wli", "tw", "dx", "dy", "dz")


def thirds(value, axis):
    high = value.astype(BF16)
    low = (value - high.astype(F32)).astype(BF16)
    return jnp.concatenate([high, low, high], axis=axis)


def dot(left, right, contract):
    return lax.dot_general(left, right, (contract, ((), ())), preferred_element_type=F32)


def even_lanes(shape):
    return lax.broadcasted_iota(jnp.int32, shape, 1) % 2 == 0


def x_forward(forces, wx):
    return dot(wx, thirds(forces, 1), ((1,), (1,)))


def x_inverse(rows, wxi):
    return dot(thirds(rows.T, 1), wxi, ((1,), (0,)))


def z_transform(rows, wz):
    pair = jnp.concatenate([rows, jnp.roll(rows, -1, axis=1)], axis=0)
    both = dot(wz, thirds(pair, 0), ((1,), (0,)))
    return jnp.where(even_lanes((N, N)), both[:N], jnp.roll(both[N:], 1, axis=1))


def y_forward(rows, wy, wl, tw):
    outer = dot(wy, thirds(rows, 0), ((1,), (0,)))
    real, imag = outer[:72], outer[72:]
    turned = jnp.concatenate([real * tw[0] + imag * tw[1], imag * tw[0] - real * tw[1]], axis=1)
    inner = dot(thirds(turned, 1), wl, ((1,), (0,)))
    return inner[:, :N], inner[:, N:]


def y_inverse(real, imag, wyi, wli, tw):
    inner = dot(thirds(jnp.concatenate([real, imag], axis=1), 1), wli, ((1,), (0,)))
    real, imag = inner[:, :N], inner[:, N:]
    turned = jnp.concatenate([real * tw[0] - imag * tw[1], imag * tw[0] + real * tw[1]], axis=0)
    return dot(wyi, thirds(turned, 0), ((1,), (0,)))


def operator_tables(dx, dy, dz):
    def rows(main, extra):
        return jnp.concatenate([main] * 8 + [extra], axis=0)

    along_x = [rows(dx[i], dx[i]) for i in range(2)]
    along_z = [rows(dz[i][:8], dz[i][8:]) for i in range(2)]
    along_y = [dy[0], dy[1]]
    squares = (
        along_x[0] * along_x[0]
        + along_x[1] * along_x[1]
        + (along_y[0] * along_y[0] + along_y[1] * along_y[1])
        + (along_z[0] * along_z[0] + along_z[1] * along_z[1])
    )
    some = squares > 0.0
    inverse = jnp.where(some, 1.0 / jnp.where(some, squares, 1.0), 0.0)
    part = lax.broadcasted_iota(jnp.int32, squares.shape, 1) // 32
    own = [
        jnp.where(part == 0, along_x[i], jnp.where(part == 1, along_y[i], jnp.where(part == 2, along_z[i], 0.0)))
        for i in range(2)
    ]
    scale = 1.0 / (N * N * N)
    alpha = inverse * jnp.where(part == 3, scale / 0.8, scale / 1.5)
    beta = inverse * inverse * (scale / 3.0)
    return own[0], own[1], alpha, beta


def operator(real, imag, own_real, own_imag, alpha, beta):
    projected = []
    for value in (own_real * real + own_imag * imag, own_real * imag - own_imag * real):
        value = value + jnp.roll(value, 64, axis=1)
        value = value + jnp.roll(value, 32, axis=1)
        projected.append(value * beta)
    return (
        real * alpha - (own_real * projected[0] - own_imag * projected[1]),
        imag * alpha - (own_real * projected[1] + own_imag * projected[0]),
    )


def kernel(adjoint, source, contrast, phase, grain, orientation, *rest):
    tables = dict(zip(CONSTANTS, rest[: len(CONSTANTS)]))
    (
        out,
        wx, wxi, wz, wzi, wy, wyi, wl, wli, tw, dx, dy, dz,
        fields, right_side,
        halo_z_out, halo_z_in, halo_y_out, halo_y_in,
        shift_z, shift_y,
        back_z_out, back_z_in, back_y_out, back_y_in,
        send1, recv1, send2, recv2, send3, recv3, send4, recv4,
        coef, own_real, own_imag, alpha, beta, potential,
        load_sems, halo_send, halo_recv, send_sems, recv_sems,
    ) = rest[len(CONSTANTS):]
    g = lax.axis_index("grp")
    s = lax.axis_index("slab")
    first = jnp.where(s == 0, 1, 0)
    corner = jnp.where((s == 0) & (g == 0), 1, 0)

    loads = [
        pltpu.make_async_copy(adjoint, fields, load_sems.at[0]),
        pltpu.make_async_copy(tables["wx"], wx, load_sems.at[1]),
        pltpu.make_async_copy(source, right_side, load_sems.at[2]),
        pltpu.make_async_copy(tables["wz"].at[first], wz, load_sems.at[3]),
        pltpu.make_async_copy(tables["wy"].at[corner], wy, load_sems.at[4]),
        pltpu.make_async_copy(tables["wl"], wl, load_sems.at[5]),
        pltpu.make_async_copy(tables["tw"], tw, load_sems.at[6]),
        pltpu.make_async_copy(tables["dx"].at[s], dx, load_sems.at[7]),
        pltpu.make_async_copy(tables["dy"], dy, load_sems.at[8]),
        pltpu.make_async_copy(tables["dz"].at[first * GRP + g], dz, load_sems.at[9]),
        pltpu.make_async_copy(tables["wli"], wli, load_sems.at[10]),
        pltpu.make_async_copy(tables["wyi"].at[corner], wyi, load_sems.at[11]),
        pltpu.make_async_copy(tables["wzi"].at[first], wzi, load_sems.at[12]),
        pltpu.make_async_copy(tables["wxi"], wxi, load_sems.at[13]),
    ]
    for load in loads:
        load.start()

    barrier = pltpu.get_barrier_semaphore()

    def greet_slab(step, carry):
        pl.semaphore_signal(
            barrier, inc=1, device_id={"slab": lax.rem(s + step, SLAB)}, device_id_type=MESH
        )
        return carry

    def greet_grp(step, carry):
        pl.semaphore_signal(
            barrier, inc=1, device_id={"grp": lax.rem(g + step, GRP)}, device_id_type=MESH
        )
        return carry

    lax.fori_loop(1, SLAB, greet_slab, 0)
    lax.fori_loop(1, GRP, greet_grp, 0)

    loads[0].wait()
    for slot, part in enumerate((4, 3, 2, 8)):
        halo_z_out[slot] = fields[part, pl.ds(1, 16, stride=2), :]
    for slot, part in enumerate((5, 1, 3, 7)):
        halo_y_out[slot] = fields[part, 30:32, :]
    pl.semaphore_wait(barrier, SLAB - 1 + GRP - 1)

    halos = [
        pltpu.make_async_remote_copy(
            halo_z_out, halo_z_in, halo_send.at[0], halo_recv.at[0],
            device_id={"slab": lax.rem(s + 1, SLAB)}, device_id_type=MESH,
        ),
        pltpu.make_async_remote_copy(
            halo_y_out, halo_y_in, halo_send.at[1], halo_recv.at[1],
            device_id={"grp": lax.rem(g + 1, GRP)}, device_id_type=MESH,
        ),
    ]
    for halo in halos:
        halo.start()

    for slot, part in enumerate((4, 3, 2, 8)):
        shift_z[slot, pl.ds(1, 16, stride=2), :] = fields[part, pl.ds(0, 16, stride=2), :]
    for slot, part in enumerate((5, 1, 3, 7)):
        shift_y[slot, 2:32, :] = fields[part, 0:30, :]

    halos[0].wait_recv()
    halos[1].wait_recv()
    for slot in range(4):
        shift_z[slot, pl.ds(0, 16, stride=2), :] = halo_z_in[slot]
        shift_y[slot, 0:2, :] = halo_y_in[slot]

    def along_x(part):
        value = fields[part]
        return jnp.roll(value, 1, axis=1) - value

    def along_y(slot):
        return shift_y[slot] - fields[(5, 1, 3, 7)[slot]]

    def along_z(slot):
        return shift_z[slot] - fields[(4, 3, 2, 8)[slot]]

    forces = jnp.concatenate(
        [
            along_x(0) + ROOT_HALF * (along_z(0) + along_y(0)),
            along_y(1) + ROOT_HALF * (along_z(1) + along_x(5)),
            along_z(2) + ROOT_HALF * (along_y(2) + along_x(4)),
            -(along_x(6) + along_y(3) + along_z(3)),
        ],
        axis=0,
    )

    loads[1].wait()
    send1[...] = x_forward(forces, wx[...]).reshape(SLAB, 2, N)

    def exchange_slab(sent, landed, which):
        def start(step, carry):
            peer = lax.rem(s + step, SLAB)
            pltpu.make_async_remote_copy(
                sent.at[peer], landed.at[s], send_sems.at[which], recv_sems.at[which],
                device_id={"slab": peer}, device_id_type=MESH,
            ).start()
            return carry

        lax.fori_loop(1, SLAB, start, 0)
        landed[s] = sent[s]

    def exchange_grp(sent, landed, which):
        def start(step, carry):
            peer = lax.rem(g + step, GRP)
            pltpu.make_async_remote_copy(
                sent.at[peer], landed.at[g], send_sems.at[which], recv_sems.at[which],
                device_id={"grp": peer}, device_id_type=MESH,
            ).start()
            return carry

        lax.fori_loop(1, GRP, start, 0)
        landed[g] = sent[g]

    def arrived(landed, which, count):
        block = landed.at[pl.ds(0, count)]
        pltpu.make_async_copy(block, block, recv_sems.at[which]).wait()

    def gone(sent, which, count):
        block = sent.at[pl.ds(0, count)]
        pltpu.make_async_copy(block, block, send_sems.at[which]).wait()

    exchange_slab(send1, recv1, 0)

    ids = grain[...]
    high, low = ids // N, ids % N
    entry = jnp.zeros((32, N), jnp.int32)
    for row in range(32):
        line = jnp.broadcast_to(orientation[row : row + 1, :], (32, N))
        entry = jnp.where(high == row, jnp.take_along_axis(line, low, axis=1), entry)
    entry = jnp.where(phase[...] == 1, entry, 6)
    masks = [entry == t for t in range(6)]
    for pair in range(81):
        value = jnp.full((32, N), contrast[6, pair], F32)
        for t in range(6):
            value = jnp.where(masks[t], contrast[t, pair], value)
        coef[pair] = value

    arrived(recv1, 0, SLAB - 1)
    loads[3].wait()
    send2[...] = z_transform(recv1[...].reshape(N, N), wz[...]).reshape(GRP, 16, N)
    exchange_grp(send2, recv2, 1)

    for load in loads[4:14]:
        load.wait()
    own_real[...], own_imag[...], alpha[...], beta[...] = operator_tables(dx, dy, dz)

    arrived(recv2, 1, GRP - 1)
    real, imag = y_forward(recv2[...].reshape(N, N), wy[...], wl[...], tw)
    real, imag = operator(real, imag, own_real[...], own_imag[...], alpha[...], beta[...])
    send3[...] = y_inverse(real, imag, wyi[...], wli[...], tw).reshape(GRP, 16, N)
    exchange_grp(send3, recv3, 2)

    arrived(recv3, 2, GRP - 1)
    send4[...] = z_transform(recv3[...].reshape(N, N), wzi[...]).reshape(SLAB, 2, N)
    exchange_slab(send4, recv4, 3)

    arrived(recv4, 3, SLAB - 1)
    potential[...] = x_inverse(recv4[...].reshape(N, N), wxi[...]).reshape(4, 32, N)

    for part in range(4):
        back_z_out[part] = potential[part, pl.ds(0, 16, stride=2), :]
        back_y_out[part] = potential[part, 0:2, :]
    backs = [
        pltpu.make_async_remote_copy(
            back_z_out, back_z_in, halo_send.at[2], halo_recv.at[2],
            device_id={"slab": lax.rem(s + SLAB - 1, SLAB)}, device_id_type=MESH,
        ),
        pltpu.make_async_remote_copy(
            back_y_out, back_y_in, halo_send.at[3], halo_recv.at[3],
            device_id={"grp": lax.rem(g + GRP - 1, GRP)}, device_id_type=MESH,
        ),
    ]
    for back in backs:
        back.start()
    for part in range(4):
        shift_z[part, pl.ds(0, 16, stride=2), :] = potential[part, pl.ds(1, 16, stride=2), :]
        shift_y[part, 0:30, :] = potential[part, 2:32, :]
    loads[2].wait()
    for back in backs:
        back.wait_recv()
    for part in range(4):
        shift_z[part, pl.ds(1, 16, stride=2), :] = back_z_in[part]
        shift_y[part, 30:32, :] = back_y_in[part]

    values = [potential[part] for part in range(4)]
    grad_x = [jnp.roll(value, N - 1, axis=1) - value for value in values]
    grad_y = [shift_y[part] - values[part] for part in range(4)]
    grad_z = [shift_z[part] - values[part] for part in range(4)]
    green = [
        grad_x[0],
        grad_y[1],
        grad_z[2],
        ROOT_HALF * (grad_y[2] + grad_z[1]),
        ROOT_HALF * (grad_x[2] + grad_z[0]),
        ROOT_HALF * (grad_x[1] + grad_y[0]),
        -grad_x[3],
        -grad_y[3],
        -grad_z[3],
    ]
    for i in range(9):
        total = right_side[i]
        for j in range(9):
            total = total - coef[j * 9 + i] * green[j]
        out[i] = total

    for halo in halos + backs:
        halo.wait_send()
    gone(send1, 0, SLAB - 1)
    gone(send2, 1, GRP - 1)
    gone(send3, 2, GRP - 1)
    gone(send4, 3, SLAB - 1)


def per_device(adjoint, source, contrast, phase_id, grain_id, orientation):
    table = constants()
    vmem = pl.BlockSpec(memory_space=pltpu.VMEM)
    smem = pl.BlockSpec(memory_space=pltpu.SMEM)
    anywhere = pl.BlockSpec(memory_space=pl.ANY)
    flat = (9, 32, N)
    result = pl.pallas_call(
        kernel,
        out_shape=jax.ShapeDtypeStruct(flat, F32),
        in_specs=[anywhere, anywhere, smem, vmem, vmem, vmem] + [anywhere] * len(CONSTANTS),
        out_specs=vmem,
        scratch_shapes=[
            pltpu.VMEM((128, 384), BF16),
            pltpu.VMEM((384, 128), BF16),
            pltpu.VMEM((256, 768), BF16),
            pltpu.VMEM((256, 768), BF16),
            pltpu.VMEM((144, 384), BF16),
            pltpu.VMEM((128, 432), BF16),
            pltpu.VMEM((768, 256), BF16),
            pltpu.VMEM((768, 256), BF16),
            pltpu.VMEM((2, 72, N), F32),
            pltpu.VMEM((2, 8, N), F32),
            pltpu.VMEM((2, 72, N), F32),
            pltpu.VMEM((2, 16, N), F32),
            pltpu.VMEM(flat, F32),
            pltpu.VMEM(flat, F32),
            pltpu.VMEM((4, 16, N), F32),
            pltpu.VMEM((4, 16, N), F32),
            pltpu.VMEM((4, 2, N), F32),
            pltpu.VMEM((4, 2, N), F32),
            pltpu.VMEM((4, 32, N), F32),
            pltpu.VMEM((4, 32, N), F32),
            pltpu.VMEM((4, 16, N), F32),
            pltpu.VMEM((4, 16, N), F32),
            pltpu.VMEM((4, 2, N), F32),
            pltpu.VMEM((4, 2, N), F32),
            pltpu.VMEM((SLAB, 2, N), F32),
            pltpu.VMEM((SLAB, 2, N), F32),
            pltpu.VMEM((GRP, 16, N), F32),
            pltpu.VMEM((GRP, 16, N), F32),
            pltpu.VMEM((GRP, 16, N), F32),
            pltpu.VMEM((GRP, 16, N), F32),
            pltpu.VMEM((SLAB, 2, N), F32),
            pltpu.VMEM((SLAB, 2, N), F32),
            pltpu.VMEM((81, 32, N), F32),
            pltpu.VMEM((72, N), F32),
            pltpu.VMEM((72, N), F32),
            pltpu.VMEM((72, N), F32),
            pltpu.VMEM((72, N), F32),
            pltpu.VMEM((4, 32, N), F32),
            pltpu.SemaphoreType.DMA((14,)),
            pltpu.SemaphoreType.DMA((4,)),
            pltpu.SemaphoreType.DMA((4,)),
            pltpu.SemaphoreType.DMA((4,)),
            pltpu.SemaphoreType.DMA((4,)),
        ],
        compiler_params=pltpu.CompilerParams(
            collective_id=0, has_side_effects=True, vmem_limit_bytes=32 * 1024 * 1024
        ),
    )(
        adjoint.reshape(flat),
        source.reshape(flat),
        contrast.reshape(7, 81),
        phase_id.reshape(32, N),
        grain_id.reshape(32, N),
        orientation.reshape(32, N),
        *[jnp.asarray(table[name]) for name in CONSTANTS],
    )
    return result.reshape(adjoint.shape)


def solution(mesh):
    placed = (
        P(None, "grp", "slab", None),
        P(None, "grp", "slab", None),
        P(),
        P("grp", "slab", None),
        P("grp", "slab", None),
        P(),
    )
    return jax.shard_map(
        per_device,
        mesh=mesh,
        in_specs=placed,
        out_specs=P(None, "grp", "slab", None),
        check_vma=False,
    )
```

profile of v0, /device:TPU:6, one launch (start us, length us, event | category | flops | bytes accessed | tf_op | source)
XLA Modules:
  0.0 82.0 jit_solution(12550184399804781716)
XLA Ops:
  0.0 0.0 copy-start.8
  0.0 0.8 copy.20
  0.8 0.0 copy-start.14
  0.8 0.1 reshape.23.contrast
  0.9 0.0 copy-done.8
  0.9 0.6 copy-done.14
  1.6 0.0 copy-start
  1.6 1.1 %copy-done = bf16[2,256,768]{2,1,0:T(8,128)(2,1)S(1)} copy-done((bf16[2,256,768]{2,1,0:T(8,128)(2,1)S(1)}, bf16[2,256,768]{2,1,0:T(8,128)(2,1)}, u32[]{:S(2)}) %copy-start) | copy-done | bytes 786456
  2.7 0.0 copy-start.1
  2.7 1.1 %copy-done.1 = bf16[2,256,768]{2,1,0:T(8,128)(2,1)S(1)} copy-done((bf16[2,256,768]{2,1,0:T(8,128)(2,1)S(1)}, bf16[2,256,768]{2,1,0:T(8,128)(2,1)}, u32[]{:S(2)}) %copy-start.1) | copy-done | bytes 786456
  3.8 0.0 copy-start.2
  3.8 1.0 %copy-done.2 = f32[64,2,8,128]{3,2,1,0:T(8,128)S(1)} copy-done((f32[64,2,8,128]{3,2,1,0:T(8,128)S(1)}, f32[64,2,8,128]{3,2,1,0:T(8,128)}, u32[]{:S(2)}) %copy-start.2) | copy-done | bytes 524312
  4.9 0.0 copy-start.3
  4.9 1.0 %copy-done.3 = bf16[768,256]{1,0:T(8,128)(2,1)S(1)} copy-done((bf16[768,256]{1,0:T(8,128)(2,1)S(1)}, bf16[768,256]{1,0:T(8,128)(2,1)}, u32[]{:S(2)}) %copy-start.3) | copy-done | bytes 393240
  5.9 0.0 copy-start.4
  5.9 1.0 %copy-done.4 = bf16[768,256]{1,0:T(8,128)(2,1)S(1)} copy-done((bf16[768,256]{1,0:T(8,128)(2,1)S(1)}, bf16[768,256]{1,0:T(8,128)(2,1)}, u32[]{:S(2)}) %copy-start.4) | copy-done | bytes 393240
  6.9 0.0 copy-start.5
  6.9 0.9 %copy-done.5 = f32[16,2,16,128]{3,2,1,0:T(8,128)S(1)} copy-done((f32[16,2,16,128]{3,2,1,0:T(8,128)S(1)}, f32[16,2,16,128]{3,2,1,0:T(8,128)}, u32[]{:S(2)}) %copy-start.5) | copy-done | bytes 262168
  7.8 0.0 copy-start.6
  7.8 0.9 %copy-done.6 = bf16[2,128,432]{2,1,0:T(8,128)(2,1)S(1)} copy-done((bf16[2,128,432]{2,1,0:T(8,128)(2,1)S(1)}, bf16[2,128,432]{2,1,0:T(8,128)(2,1)}, u32[]{:S(2)}) %copy-start.6) | copy-done | bytes 221208
  8.8 0.0 copy-start.7
  8.8 0.9 %copy-done.7 = bf16[2,144,384]{2,1,0:T(8,128)(2,1)S(1)} copy-done((bf16[2,144,384]{2,1,0:T(8,128)(2,1)S(1)}, bf16[2,144,384]{2,1,0:T(8,128)(2,1)}, u32[]{:S(2)}) %copy-start.7) | copy-done | bytes 221208
  9.7 0.0 copy-start.9
  9.7 0.9 %copy-done.9 = f32[9,16,2,128]{3,2,1,0:T(2,128)S(1)} copy-done((f32[9,16,2,128]{3,2,1,0:T(2,128)S(1)}, f32[9,16,2,128]{3,2,1,0:T(2,128)}, u32[]{:S(2)}) %copy-start.9) | copy-done | bytes 147480
  10.6 0.0 copy-start.10
  10.6 0.9 %copy-done.10 = bf16[384,128]{1,0:T(8,128)(2,1)S(1)} copy-done((bf16[384,128]{1,0:T(8,128)(2,1)S(1)}, bf16[384,128]{1,0:T(8,128)(2,1)}, u32[]{:S(2)}) %copy-start.10) | copy-done | bytes 98328
  11.5 0.0 copy-start.11
  11.5 0.9 %copy-done.11 = bf16[128,384]{1,0:T(8,128)(2,1)S(1)} copy-done((bf16[128,384]{1,0:T(8,128)(2,1)S(1)}, bf16[128,384]{1,0:T(8,128)(2,1)}, u32[]{:S(2)}) %copy-start.11) | copy-done | bytes 98328
  12.4 0.0 copy-start.12
  12.4 0.9 %copy-done.12 = f32[2,72,128]{2,1,0:T(8,128)S(1)} copy-done((f32[2,72,128]{2,1,0:T(8,128)S(1)}, f32[2,72,128]{2,1,0:T(8,128)}, u32[]{:S(2)}) %copy-start.12) | copy-done | bytes 73752
  13.3 0.0 copy-start.13
  13.3 0.9 %copy-done.13 = f32[2,72,128]{2,1,0:T(8,128)S(1)} copy-done((f32[2,72,128]{2,1,0:T(8,128)S(1)}, f32[2,72,128]{2,1,0:T(8,128)}, u32[]{:S(2)}) %copy-start.13) | copy-done | bytes 73752
  14.2 0.0 copy-start.15
  14.2 0.7 copy-done.15
  14.9 0.0 copy-start.16
  14.9 0.7 copy-done.16
  15.6 65.7 %shard_map.172 = f32[9,32,128]{2,1,0:T(8,128)S(1)} custom-call(f32[9,32,128]{2,1,0:T(8,128)S(1)} %bitcast.7, f32[9,32,128]{2,1,0:T(8,128)S(1)} %bitcast.8, f32[7,81]{1,0:T(8,128)S(1)} %reshape.23.contrast, s32[32,128]{1,0:T(8,128)S(1)} %bitcast.9, s32[32,128]{1,0:T(8,128)S(1)} %bitcast.10, s32[32,128]{1,0:T(8,128)S(1)} %bitcast.11, ...), custom_call_target="tpu_custom_call" | custom-call | tf_op jit(solution)/shard_map/pallas_call | solution.py:503
  81.3 0.7 copy.22
Async XLA Ops:
  0.0 0.9 %copy-start.8 = (f32[9,16,2,128]{3,2,1,0:T(2,128)S(1)}, f32[9,16,2,128]{3,2,1,0:T(2,128)}, u32[]{:S(2)}) copy-start(f32[9,16,2,128]{3,2,1,0:T(2,128)} %param.18) | copy-start | bytes 442372
  0.8 0.7 copy-start.14
  1.6 1.1 %copy-start = (bf16[2,256,768]{2,1,0:T(8,128)(2,1)S(1)}, bf16[2,256,768]{2,1,0:T(8,128)(2,1)}, u32[]{:S(2)}) copy-start(bf16[2,256,768]{2,1,0:T(8,128)(2,1)} %constant.27.clone.rest_3_) | copy-start | bytes 2359300
  2.7 1.1 %copy-start.1 = (bf16[2,256,768]{2,1,0:T(8,128)(2,1)S(1)}, bf16[2,256,768]{2,1,0:T(8,128)(2,1)}, u32[]{:S(2)}) copy-start(bf16[2,256,768]{2,1,0:T(8,128)(2,1)} %constant.26.clone.rest_2_) | copy-start | bytes 2359300
  3.8 1.0 %copy-start.2 = (f32[64,2,8,128]{3,2,1,0:T(8,128)S(1)}, f32[64,2,8,128]{3,2,1,0:T(8,128)}, u32[]{:S(2)}) copy-start(f32[64,2,8,128]{3,2,1,0:T(8,128)} %constant.33.clone.rest_9_) | copy-start | bytes 1572868
  4.9 1.0 %copy-start.3 = (bf16[768,256]{1,0:T(8,128)(2,1)S(1)}, bf16[768,256]{1,0:T(8,128)(2,1)}, u32[]{:S(2)}) copy-start(bf16[768,256]{1,0:T(8,128)(2,1)} %constant.31.clone.rest_7_) | copy-start | bytes 1179652
  5.9 1.0 %copy-start.4 = (bf16[768,256]{1,0:T(8,128)(2,1)S(1)}, bf16[768,256]{1,0:T(8,128)(2,1)}, u32[]{:S(2)}) copy-start(bf16[768,256]{1,0:T(8,128)(2,1)} %constant.30.clone.rest_6_) | copy-start | bytes 1179652
  6.9 0.9 %copy-start.5 = (f32[16,2,16,128]{3,2,1,0:T(8,128)S(1)}, f32[16,2,16,128]{3,2,1,0:T(8,128)}, u32[]{:S(2)}) copy-start(f32[16,2,16,128]{3,2,1,0:T(8,128)} %constant.35.clone.rest_11_) | copy-start | bytes 786436
  7.8 0.9 %copy-start.6 = (bf16[2,128,432]{2,1,0:T(8,128)(2,1)S(1)}, bf16[2,128,432]{2,1,0:T(8,128)(2,1)}, u32[]{:S(2)}) copy-start(bf16[2,128,432]{2,1,0:T(8,128)(2,1)} %constant.29.clone.rest_5_) | copy-start | bytes 663556
  8.8 0.9 %copy-start.7 = (bf16[2,144,384]{2,1,0:T(8,128)(2,1)S(1)}, bf16[2,144,384]{2,1,0:T(8,128)(2,1)}, u32[]{:S(2)}) copy-start(bf16[2,144,384]{2,1,0:T(8,128)(2,1)} %constant.28.clone.rest_4_) | copy-start | bytes 663556
  9.7 0.9 %copy-start.9 = (f32[9,16,2,128]{3,2,1,0:T(2,128)S(1)}, f32[9,16,2,128]{3,2,1,0:T(2,128)}, u32[]{:S(2)}) copy-start(f32[9,16,2,128]{3,2,1,0:T(2,128)} %param.19) | copy-start | bytes 442372
  10.6 0.9 %copy-start.10 = (bf16[384,128]{1,0:T(8,128)(2,1)S(1)}, bf16[384,128]{1,0:T(8,128)(2,1)}, u32[]{:S(2)}) copy-start(bf16[384,128]{1,0:T(8,128)(2,1)} %constant.25.clone.rest_1_) | copy-start | bytes 294916
  11.5 0.9 %copy-start.11 = (bf16[128,384]{1,0:T(8,128)(2,1)S(1)}, bf16[128,384]{1,0:T(8,128)(2,1)}, u32[]{:S(2)}) copy-start(bf16[128,384]{1,0:T(8,128)(2,1)} %constant.24.clone.rest_0_) | copy-start | bytes 294916
  12.4 0.9 %copy-start.12 = (f32[2,72,128]{2,1,0:T(8,128)S(1)}, f32[2,72,128]{2,1,0:T(8,128)}, u32[]{:S(2)}) copy-start(f32[2,72,128]{2,1,0:T(8,128)} %constant.34.clone.rest_10_) | copy-start | bytes 221188
  13.3 0.9 %copy-start.13 = (f32[2,72,128]{2,1,0:T(8,128)S(1)}, f32[2,72,128]{2,1,0:T(8,128)}, u32[]{:S(2)}) copy-start(f32[2,72,128]{2,1,0:T(8,128)} %constant.32.clone.rest_8_) | copy-start | bytes 221188
  14.2 0.7 copy-start.15
  14.9 0.7 copy-start.16
where the time goes:
time: 82.7 us; the launch traced here: 82 us
  Pallas kernels  65.7 us (79%)
  local copies, waits for them, and re-layouts  16.2 us (20%)
    pallas_call x1, Pallas kernels, per_device(): pl.pallas_call(kernel, out_shape=jax.ShapeDtypeStruct(flat, F32), in_spec...  65.7 us
    unnamed x36, local copies, waits for them, and re-layouts  16.2 us

commit v1 on v0

v1 whole, which is shorter than its diff:
```python
import functools

import jax
import jax.numpy as jnp
import ml_dtypes
import numpy as np
from jax import lax
from jax.experimental import pallas as pl
from jax.experimental.pallas import tpu as pltpu
from jax.sharding import PartitionSpec as P

N = 128
GRP = 8
SLAB = 64
F32 = jnp.float32
BF16 = jnp.bfloat16
ROOT_HALF = float(np.sqrt(0.5))
MESH = pl.DeviceIdType.MESH


def split_const(matrix, axis):
    high = matrix.astype(ml_dtypes.bfloat16)
    low = (matrix - high.astype(np.float64)).astype(ml_dtypes.bfloat16)
    return np.concatenate([high, high, low], axis=axis)


def angle(a, b, length=N):
    return 2.0 * np.pi * ((np.asarray(a) * np.asarray(b)) % length) / length


def x_tables():
    x = np.arange(N)
    forward = np.zeros((SLAB, 2, N))
    inverse = np.zeros((SLAB, 2, N))
    for k in range(1, SLAB):
        forward[k, 0] = np.cos(angle(k, x))
        forward[k, 1] = -np.sin(angle(k, x))
    forward[0, 0] = 1.0
    forward[0, 1] = (-1.0) ** x
    inverse[1:] = 2.0 * forward[1:]
    inverse[0] = forward[0]
    return forward.reshape(N, N), inverse.reshape(N, N)


def z_tables(first):
    z = (2 * np.arange(SLAB)[:, None] + np.arange(3)[None, :]) % N
    forward = np.zeros((2, GRP, 2, 8, 3, SLAB, 2))
    inverse = np.zeros((3, SLAB, 2, 2, GRP, 2, 8))
    for m in range(SLAB):
        hi, lo = divmod(m, 8)
        for h in range(2):
            for z2 in range(3):
                if first:
                    cos, sin = np.cos(angle(m, z[:, z2])), np.sin(angle(m, z[:, z2]))
                    if m == 0:
                        alt = (-1.0) ** z[:, z2]
                        forward[h, hi, 0, lo, z2, :, h] = 1.0
                        forward[h, hi, 1, lo, z2, :, h] = alt
                        inverse[z2, :, h, h, hi, 0, lo] = 1.0
                        inverse[z2, :, h, h, hi, 1, lo] = alt
                    else:
                        forward[h, hi, 0, lo, z2, :, h] = cos
                        forward[h, hi, 1, lo, z2, :, h] = -sin
                        inverse[z2, :, h, h, hi, 0, lo] = 2.0 * cos
                        inverse[z2, :, h, h, hi, 1, lo] = -2.0 * sin
                else:
                    k = m if h == 0 else (64 if m == 0 else N - m)
                    cos, sin = np.cos(angle(k, z[:, z2])), np.sin(angle(k, z[:, z2]))
                    forward[h, hi, 0, lo, z2, :, 0] = cos
                    forward[h, hi, 0, lo, z2, :, 1] = sin
                    forward[h, hi, 1, lo, z2, :, 0] = -sin
                    forward[h, hi, 1, lo, z2, :, 1] = cos
                    inverse[z2, :, 0, h, hi, 0, lo] = cos
                    inverse[z2, :, 0, h, hi, 1, lo] = -sin
                    inverse[z2, :, 1, h, hi, 0, lo] = sin
                    inverse[z2, :, 1, h, hi, 1, lo] = cos
    return forward.reshape(256, 384), inverse.reshape(384, 256)


def y_outer_tables(corner):
    forward = np.zeros((2, 72, GRP, 2, 8))
    inverse = np.zeros((GRP, 2, 8, 2, 72))
    g = np.arange(GRP)
    for k1 in range(8):
        cos, sin = np.cos(angle(k1, g, 8)), np.sin(angle(k1, g, 8))
        for kz in range(8):
            row = k1 * 8 + kz
            if corner and kz == 0:
                for source, target in ((0, row), (1, 64 + k1)):
                    forward[0, target, :, source, kz] = cos
                    forward[1, target, :, source, kz] = -sin
                    inverse[:, source, kz, 0, target] = cos
                    inverse[:, source, kz, 1, target] = -sin
            else:
                forward[0, row, :, 0, kz] = cos
                forward[0, row, :, 1, kz] = sin
                forward[1, row, :, 0, kz] = -sin
                forward[1, row, :, 1, kz] = cos
                inverse[:, 0, kz, 0, row] = cos
                inverse[:, 0, kz, 1, row] = -sin
                inverse[:, 1, kz, 0, row] = sin
                inverse[:, 1, kz, 1, row] = cos
    return forward.reshape(144, 128), inverse.reshape(128, 144)


def y_edge_tables():
    turn = angle(np.arange(8)[:, None], np.arange(8)[None, :] + 1, 8)
    forward = np.zeros((2, 2, 8, 8, 2))
    for ri in range(2):
        forward[ri, 0, :, :, ri] = np.cos(turn)
        forward[ri, 1, :, :, ri] = np.sin(turn)
    inverse = np.concatenate([np.cos(turn).T, np.sin(turn).T])
    return forward.reshape(32, 16).astype(np.float32), inverse.astype(np.float32)


def lane_parts():
    lane = np.arange(N)
    return lane // 16 % 4, lane % 16, lane // 64


def edge_parts():
    lane = np.arange(N)
    return lane // 8 % 4, lane // 32 % 2, lane // 64


def y_inner_tables():
    c, y, h = lane_parts()
    same = (c[:, None] == c[None, :]) & (h[:, None] == h[None, :])
    cos = np.where(same, np.cos(angle(y[:, None], y[None, :], 16)), 0.0)
    sin = np.where(same, np.sin(angle(y[:, None], y[None, :], 16)), 0.0)
    edge_c, edge_h, edge_real = edge_parts()
    meet = (edge_c[:, None] == c[None, :]) & (edge_h[:, None] == h[None, :])
    to_real = (meet & (edge_real[:, None] == 1)).astype(np.float64)
    to_imag = (meet & (edge_real[:, None] == 0)).astype(np.float64)
    forward = np.block([[cos, -sin], [sin, cos], [to_real, to_imag]])
    inverse = np.block([[cos, sin, to_real.T], [-sin, cos, to_imag.T]])
    return forward, inverse


def row_k1():
    return np.concatenate([np.repeat(np.arange(8), 8), np.arange(8)])


def twiddle_tables():
    _, y, _ = lane_parts()
    turn = angle(row_k1()[:, None], y[None, :])
    return np.stack([np.cos(turn), np.sin(turn)]).astype(np.float32)


def symbol(k):
    turn = 2.0 * np.pi * (np.asarray(k) % N) / N
    return np.stack([np.cos(turn) - 1.0, np.sin(turn)]).astype(np.float32)


def symbol_tables():
    _, k2, h = lane_parts()
    along_y = symbol(row_k1()[:, None] + 8 * k2[None, :])
    along_x = np.zeros((SLAB, 2, 8, N), np.float32)
    for s in range(SLAB):
        k = np.where(h == 0, 0, 64) if s == 0 else np.full(N, s)
        along_x[s] = np.broadcast_to(symbol(k)[:, None, :], (2, 8, N))
    along_z = np.zeros((2 * GRP, 2, 16, N), np.float32)
    for first in range(2):
        for g in range(GRP):
            for row in range(16):
                m = g * 8 + row
                if row >= 8:
                    k = np.full(N, 64)
                elif first:
                    k = np.full(N, m)
                else:
                    k = np.where(h == 0, m, 64 if m == 0 else N - m)
                along_z[first * GRP + g, :, row] = symbol(k)
    return along_x, along_y, along_z


@functools.cache
def constants():
    x_forward, x_inverse = x_tables()
    z_pairs = [z_tables(first) for first in (False, True)]
    y_pairs = [y_outer_tables(corner) for corner in (False, True)]
    inner_forward, inner_inverse = y_inner_tables()
    along_x, along_y, along_z = symbol_tables()
    return dict(
        wx=split_const(x_forward, 1),
        wxi=split_const(x_inverse, 0),
        wz=np.stack([split_const(pair[0], 1) for pair in z_pairs]),
        wzi=np.stack([split_const(pair[1], 1) for pair in z_pairs]),
        wy=np.stack([split_const(pair[0], 1) for pair in y_pairs]),
        wyi=np.stack([split_const(pair[1], 1) for pair in y_pairs]),
        wl=split_const(inner_forward, 0),
        wli=split_const(inner_inverse, 0),
        we=y_edge_tables()[0],
        wei=y_edge_tables()[1],
        tw=twiddle_tables(),
        dx=along_x,
        dy=along_y,
        dz=along_z,
    )


CONSTANTS = ("wx", "wxi", "wz", "wzi", "wy", "wyi", "wl", "wli", "we", "wei", "tw", "dx", "dy", "dz")


def thirds(value, axis):
    high = value.astype(BF16)
    low = (value - high.astype(F32)).astype(BF16)
    return jnp.concatenate([high, low, high], axis=axis)


def dot(left, right, contract):
    return lax.dot_general(left, right, (contract, ((), ())), preferred_element_type=F32)


def lanes(shape):
    return lax.broadcasted_iota(jnp.int32, shape, len(shape) - 1)


def sublanes(shape):
    return lax.broadcasted_iota(jnp.int32, shape, len(shape) - 2)


def force_lines(take):
    edge = sublanes((16, N)) == 0

    def along_x(part, z2):
        value = take(part, z2)
        return jnp.roll(value, 1, axis=1) - value

    def along_y(part, z2):
        value = take(part, z2)
        return jnp.where(edge, 0.0, jnp.roll(value, 1, axis=0)) - value

    def along_z(part, z2):
        return take(part, 0) - take(part, 1) if z2 == 1 else -take(part, 0)

    lines = []
    for z2 in range(2):
        lines += [
            along_x(0, z2) + ROOT_HALF * (along_z(4, z2) + along_y(5, z2)),
            along_y(1, z2) + ROOT_HALF * (along_z(3, z2) + along_x(5, z2)),
            along_z(2, z2) + ROOT_HALF * (along_y(3, z2) + along_x(4, z2)),
            -(along_x(6, z2) + along_y(7, z2) + along_z(8, z2)),
        ]
    lines += [ROOT_HALF * take(4, 1), ROOT_HALF * take(3, 1), take(2, 1), -take(8, 1)]
    for z2 in range(2):
        for scale, part in ((ROOT_HALF, 5), (1.0, 1), (ROOT_HALF, 3), (-1.0, 7)):
            lines.append(jnp.broadcast_to(scale * take(part, z2)[15:16], (8, N)))
    return jnp.concatenate(lines, axis=0)


def x_forward(lines, wx):
    return dot(wx, thirds(lines, 1), ((1,), (1,)))


def x_inverse(rows, wxi):
    return dot(thirds(rows.T, 1), wxi, ((1,), (0,)))


def z_forward(rows, wz):
    lane = lanes((N, N))
    low = lane < 64
    main, rest = rows[:, :N], rows[:, N:]
    parts = jnp.concatenate(
        [
            jnp.where(low, main, rest),
            jnp.where(low, jnp.roll(main, 64, axis=1), jnp.roll(rest, 96, axis=1)),
            jnp.where(low, rest, 0.0),
        ],
        axis=0,
    )
    both = dot(wz, thirds(parts, 0), ((1,), (0,)))
    first, second = both[:N], both[N:]
    edge = jnp.where(lane < 96, first, jnp.roll(second, 32, axis=1))
    edge = jnp.where((lane % 8 == sublanes((N, N)) % 8) & (lane >= 64), edge, 0.0)
    return jnp.where(low, first, jnp.roll(second, 64, axis=1)), edge.reshape(16, 8, N).sum(axis=1)


def z_inverse(rows, edge, wzi):
    lane = lanes((N, N))
    low = lane < 64
    edge = jnp.broadcast_to(edge[:, None, :], (16, 8, N)).reshape(N, N)
    edge = jnp.where(lane % 8 == sublanes((N, N)) % 8, edge, 0.0)
    parts = jnp.concatenate(
        [jnp.where(low, rows, edge), jnp.where(low, jnp.roll(rows, 64, axis=1), jnp.roll(edge, 96, axis=1))], axis=0
    )
    planes = dot(wzi, thirds(parts, 0), ((1,), (0,)))
    first, second, third = planes[:N], planes[N : 2 * N], planes[2 * N :]
    main = jnp.where(low, first, jnp.roll(second, 64, axis=1))
    rest = jnp.where(low, third, jnp.where(lane < 96, first, jnp.roll(second, 32, axis=1)))
    return jnp.concatenate([main, rest], axis=1)


def exact_dot(left, right):
    return lax.dot_general(
        left, right, (((1,), (0,)), ((), ())), precision=lax.Precision.HIGHEST, preferred_element_type=F32
    )


def y_forward(rows, edge, corner, wy, wl, we, tw):
    outer = dot(wy, thirds(rows, 0), ((1,), (0,)))
    real, imag = outer[:72], outer[72:]
    turns = exact_dot(we, edge)
    lane = lanes((8, N))
    packed = (lane % 8 == 0) & (corner == 1)
    edge_real = turns[:8] + jnp.where(packed, 0.0, turns[24:])
    edge_imag = jnp.where(packed, 0.0, turns[16:24]) - turns[8:16]
    mixed = jnp.where(lane < 64, jnp.roll(edge_imag, 64, axis=1), edge_real)
    extra = jnp.where(packed, jnp.where(lane < 64, -jnp.roll(turns[24:], 64, axis=1), turns[16:24]), 0.0)
    spread = jnp.broadcast_to(mixed[:, None, :], (8, 8, N)).reshape(64, N)
    spread = jnp.where(lanes((64, N)) % 8 == sublanes((64, N)) % 8, spread, 0.0)
    turned = jnp.concatenate(
        [real * tw[0] + imag * tw[1], imag * tw[0] - real * tw[1], jnp.concatenate([spread, extra], axis=0)], axis=1
    )
    inner = dot(thirds(turned, 1), wl, ((1,), (0,)))
    return inner[:, :N], inner[:, N:]


def y_inverse(real, imag, corner, wyi, wli, wei, tw):
    inner = dot(thirds(jnp.concatenate([real, imag], axis=1), 1), wli, ((1,), (0,)))
    real, imag, mixed = inner[:, :N], inner[:, N : 2 * N], inner[:, 2 * N :]
    turned = jnp.concatenate([real * tw[0] - imag * tw[1], imag * tw[0] + real * tw[1]], axis=0)
    rows = dot(wyi, thirds(turned, 0), ((1,), (0,)))
    lane = lanes((8, N))
    packed = (lane % 8 == 0) & (corner == 1)
    spread = jnp.where(lanes((64, N)) % 8 == sublanes((64, N)) % 8, mixed[:64], 0.0)
    turns = exact_dot(wei, jnp.concatenate([spread.reshape(8, 8, N).sum(axis=1), mixed[64:]], axis=1))
    edge_real = turns[:8, :N] - jnp.roll(turns[8:, :N], 64, axis=1)
    edge_imag = turns[8:, :N] + jnp.roll(turns[:8, :N], 64, axis=1)
    extra = turns[:8, N:] - jnp.roll(turns[8:, N:], 64, axis=1)
    return rows, edge_real, jnp.where(packed, extra, edge_imag)


def gradients(lines):
    last = sublanes((16, N)) == 15
    grad_x, grad_y, grad_z = [], [], []
    for c in range(4):
        along = [[], [], []]
        for z2 in range(2):
            start = z2 * 64 + c * 16
            value = lines[start : start + 16]
            above = lines[start + 64 : start + 80]
            begin = 192 + z2 * 32 + c * 8
            edge = jnp.sum(lines[begin : begin + 8], axis=0, keepdims=True)
            along[0].append(jnp.roll(value, N - 1, axis=1) - value)
            along[1].append(jnp.where(last, edge, jnp.roll(value, 15, axis=0)) - value)
            along[2].append(above - value)
        for grad, pair in zip((grad_x, grad_y, grad_z), along):
            grad.append(jnp.concatenate(pair, axis=0))
    return [
        grad_x[0],
        grad_y[1],
        grad_z[2],
        ROOT_HALF * (grad_y[2] + grad_z[1]),
        ROOT_HALF * (grad_x[2] + grad_z[0]),
        ROOT_HALF * (grad_x[1] + grad_y[0]),
        -grad_x[3],
        -grad_y[3],
        -grad_z[3],
    ]


def operator_tables(dx, dy, dz):
    def rows(main, extra):
        return jnp.concatenate([main] * 8 + [extra], axis=0)

    along_x = [rows(dx[i], dx[i]) for i in range(2)]
    along_z = [rows(dz[i][:8], dz[i][8:]) for i in range(2)]
    along_y = [dy[0], dy[1]]
    squares = (
        along_x[0] * along_x[0]
        + along_x[1] * along_x[1]
        + (along_y[0] * along_y[0] + along_y[1] * along_y[1])
        + (along_z[0] * along_z[0] + along_z[1] * along_z[1])
    )
    some = squares > 0.0
    inverse = jnp.where(some, 1.0 / jnp.where(some, squares, 1.0), 0.0)
    part = lanes(squares.shape) // 16 % 4
    own = [
        jnp.where(part == 0, along_x[i], jnp.where(part == 1, along_y[i], jnp.where(part == 2, along_z[i], 0.0)))
        for i in range(2)
    ]
    scale = 1.0 / (N * N * N)
    alpha = inverse * jnp.where(part == 3, scale / 0.8, scale / 1.5)
    beta = inverse * inverse * (scale / 3.0)
    return own[0], own[1], alpha, beta


def operator(real, imag, own_real, own_imag, alpha, beta):
    projected = []
    lane = lanes(real.shape)
    for value in (own_real * real + own_imag * imag, own_real * imag - own_imag * real):
        for width in (32, 16):
            lower = lane % (2 * width) < width
            value = value + jnp.where(lower, jnp.roll(value, N - width, axis=1), jnp.roll(value, width, axis=1))
        projected.append(value * beta)
    return (
        real * alpha - (own_real * projected[0] - own_imag * projected[1]),
        imag * alpha - (own_real * projected[1] + own_imag * projected[0]),
    )


def kernel(adjoint, source, contrast_in, phase_in, grain_in, orientation_in, *rest):
    tables = dict(zip(CONSTANTS, rest[: len(CONSTANTS)]))
    (
        out,
        wx, wxi, wz, wzi, wy, wyi, wl, wli, we, wei, tw, dx, dy, dz,
        fields, right_side, contrast, phase, grain, orientation,
        send1, recv1, send2, recv2, send3, recv3, send4, recv4,
        coef, own_real, own_imag, alpha, beta,
        load_sems, send_sems, recv_sems,
    ) = rest[len(CONSTANTS):]
    g = lax.axis_index("grp")
    s = lax.axis_index("slab")
    first = jnp.where(s == 0, 1, 0)
    corner = jnp.where((s == 0) & (g == 0), 1, 0)

    pairs = [
        (adjoint, fields),
        (tables["wx"], wx),
        (orientation_in, orientation),
        (grain_in, grain),
        (phase_in, phase),
        (contrast_in, contrast),
        (tables["wz"].at[first], wz),
        (tables["dx"].at[s], dx),
        (tables["dy"], dy),
        (tables["dz"].at[first * GRP + g], dz),
        (tables["wy"].at[corner], wy),
        (tables["wl"], wl),
        (tables["we"], we),
        (tables["tw"], tw),
        (tables["wli"], wli),
        (tables["wyi"].at[corner], wyi),
        (tables["wei"], wei),
        (tables["wzi"].at[first], wzi),
        (tables["wxi"], wxi),
        (source, right_side),
    ]
    loads = [pltpu.make_async_copy(*pair, load_sems.at[i]) for i, pair in enumerate(pairs)]
    for load in loads:
        load.start()

    digit_y, digit_z, digit_x = s // 16, lax.rem(s // 4, 4), lax.rem(s, 4)

    def slab_peers(visit):
        for step_z in (2, 1, 3, 0):
            base = lax.rem(digit_z + step_z, 4) * 4

            def row(step_y, carry):
                start = lax.rem(digit_y + step_y, 4) * 16 + base
                for step_x in range(4):
                    visit(start + lax.rem(digit_x + step_x, 4))
                return carry

            if step_z == 0:
                for step_x in range(1, 4):
                    visit(digit_y * 16 + base + lax.rem(digit_x + step_x, 4))
            lax.fori_loop(1 if step_z == 0 else 0, 4, row, 0)

    def grp_peers(visit):
        def one(step, carry):
            visit(lax.rem(g + step, GRP))
            return carry

        lax.fori_loop(1, GRP, one, 0)

    barrier = pltpu.get_barrier_semaphore()
    slab_peers(lambda peer: pl.semaphore_signal(barrier, inc=1, device_id={"slab": peer}, device_id_type=MESH))
    grp_peers(lambda peer: pl.semaphore_signal(barrier, inc=1, device_id={"grp": peer}, device_id_type=MESH))

    def exchange_slab(sent, landed, which):
        def start(peer):
            pltpu.make_async_remote_copy(
                sent.at[peer], landed.at[s], send_sems.at[which], recv_sems.at[which],
                device_id={"slab": peer}, device_id_type=MESH,
            ).start()

        slab_peers(start)
        landed[s] = sent[s]

    def exchange_grp(sent, landed, which):
        def start(peer):
            pltpu.make_async_remote_copy(
                sent.at[peer], landed.at[g], send_sems.at[which], recv_sems.at[which],
                device_id={"grp": peer}, device_id_type=MESH,
            ).start()

        grp_peers(start)
        landed[g] = sent[g]

    def arrived(landed, which, count):
        block = landed.at[pl.ds(0, count)]
        pltpu.make_async_copy(block, block, recv_sems.at[which]).wait()

    def gone(sent, which, count):
        block = sent.at[pl.ds(0, count)]
        pltpu.make_async_copy(block, block, send_sems.at[which]).wait()

    loads[0].wait()
    lines = force_lines(lambda part, z2: fields[part, pl.ds(z2, 16, stride=2), :])
    loads[1].wait()
    send1[...] = x_forward(lines, wx[...]).reshape(SLAB, 2, 2 * N)
    pl.semaphore_wait(barrier, SLAB - 1 + GRP - 1)
    exchange_slab(send1, recv1, 0)

    for load in loads[2:6]:
        load.wait()
    ids = jnp.concatenate([grain[pl.ds(z2, 16, stride=2), :] for z2 in range(2)], axis=0)
    high, low = ids // N, ids % N
    entry = jnp.zeros((32, N), jnp.int32)
    for row in range(32):
        line = jnp.broadcast_to(orientation[row : row + 1, :], (32, N))
        entry = jnp.where(high == row, jnp.take_along_axis(line, low, axis=1), entry)
    ceramic = jnp.concatenate([phase[pl.ds(z2, 16, stride=2), :] for z2 in range(2)], axis=0) == 1
    entry = jnp.where(ceramic, entry, 6)
    masks = [entry == t for t in range(6)]
    for pair in range(81):
        value = jnp.full((32, N), contrast[pair // 9, 6, pair % 9], F32)
        for t in range(6):
            value = jnp.where(masks[t], contrast[pair // 9, t, pair % 9], value)
        coef[pair] = value
    for load in loads[6:]:
        load.wait()
    own_real[...], own_imag[...], alpha[...], beta[...] = operator_tables(dx, dy, dz)

    arrived(recv1, 0, SLAB - 1)
    rows, edge = z_forward(recv1[...].reshape(N, 2 * N), wz[...])
    send2[:, 0:16, :] = rows.reshape(GRP, 16, N)
    send2[:, 16:18, :] = edge.reshape(GRP, 2, N)
    exchange_grp(send2, recv2, 1)

    arrived(recv2, 1, GRP - 1)
    real, imag = y_forward(
        recv2[:, 0:16, :].reshape(N, N), recv2[:, 16:18, :].reshape(16, N), corner, wy[...], wl[...], we[...], tw
    )
    real, imag = operator(real, imag, own_real[...], own_imag[...], alpha[...], beta[...])
    rows, edge_real, edge_imag = y_inverse(real, imag, corner, wyi[...], wli[...], wei[...], tw)
    send3[:, 0:16, :] = rows.reshape(GRP, 16, N)
    send3[:, 16:17, :] = edge_real.reshape(GRP, 1, N)
    send3[:, 17:18, :] = edge_imag.reshape(GRP, 1, N)
    exchange_grp(send3, recv3, 2)

    arrived(recv3, 2, GRP - 1)
    send4[...] = z_inverse(
        recv3[:, 0:16, :].reshape(N, N), recv3[:, 16:18, :].reshape(16, N), wzi[...]
    ).reshape(SLAB, 2, 2 * N)
    exchange_slab(send4, recv4, 3)

    arrived(recv4, 3, SLAB - 1)
    green = gradients(x_inverse(recv4[...].reshape(N, 2 * N), wxi[...]))
    for i in range(9):
        total = jnp.concatenate([right_side[i, pl.ds(z2, 16, stride=2), :] for z2 in range(2)], axis=0)
        for j in range(9):
            total = total - coef[j * 9 + i] * green[j]
        for z2 in range(2):
            out[i, pl.ds(z2, 16, stride=2), :] = total[z2 * 16 : z2 * 16 + 16]

    gone(send1, 0, SLAB - 1)
    gone(send2, 1, GRP - 1)
    gone(send3, 2, GRP - 1)
    gone(send4, 3, SLAB - 1)


def per_device(adjoint, source, contrast, phase_id, grain_id, orientation):
    table = constants()
    vmem = pl.BlockSpec(memory_space=pltpu.VMEM)
    hbm = pl.BlockSpec(memory_space=pltpu.HBM)
    flat = (9, 32, N)
    result = pl.pallas_call(
        kernel,
        out_shape=jax.ShapeDtypeStruct(flat, F32),
        in_specs=[hbm] * (6 + len(CONSTANTS)),
        out_specs=vmem,
        scratch_shapes=[
            pltpu.VMEM((128, 384), BF16),
            pltpu.VMEM((384, 128), BF16),
            pltpu.VMEM((256, 1152), BF16),
            pltpu.VMEM((384, 768), BF16),
            pltpu.VMEM((144, 384), BF16),
            pltpu.VMEM((128, 432), BF16),
            pltpu.VMEM((1152, 256), BF16),
            pltpu.VMEM((768, 384), BF16),
            pltpu.VMEM((32, 16), F32),
            pltpu.VMEM((16, 8), F32),
            pltpu.VMEM((2, 72, N), F32),
            pltpu.VMEM((2, 8, N), F32),
            pltpu.VMEM((2, 72, N), F32),
            pltpu.VMEM((2, 16, N), F32),
            pltpu.VMEM(flat, F32),
            pltpu.VMEM(flat, F32),
            pltpu.SMEM((9, 7, 9), F32),
            pltpu.VMEM((32, N), jnp.int32),
            pltpu.VMEM((32, N), jnp.int32),
            pltpu.VMEM((32, N), jnp.int32),
            pltpu.VMEM((SLAB, 2, 2 * N), F32),
            pltpu.VMEM((SLAB, 2, 2 * N), F32),
            pltpu.VMEM((GRP, 24, N), F32),
            pltpu.VMEM((GRP, 24, N), F32),
            pltpu.VMEM((GRP, 24, N), F32),
            pltpu.VMEM((GRP, 24, N), F32),
            pltpu.VMEM((SLAB, 2, 2 * N), F32),
            pltpu.VMEM((SLAB, 2, 2 * N), F32),
            pltpu.VMEM((81, 32, N), F32),
            pltpu.VMEM((72, N), F32),
            pltpu.VMEM((72, N), F32),
            pltpu.VMEM((72, N), F32),
            pltpu.VMEM((72, N), F32),
            pltpu.SemaphoreType.DMA((20,)),
            pltpu.SemaphoreType.DMA((4,)),
            pltpu.SemaphoreType.DMA((4,)),
        ],
        compiler_params=pltpu.CompilerParams(
            collective_id=0, has_side_effects=True, vmem_limit_bytes=60 * 1024 * 1024
        ),
    )(
        adjoint.reshape(flat),
        source.reshape(flat),
        contrast.transpose(1, 0, 2),
        phase_id.reshape(32, N),
        grain_id.reshape(32, N),
        orientation.reshape(32, N),
        *[jnp.asarray(table[name]) for name in CONSTANTS],
    )
    return result.reshape(adjoint.shape)


def solution(mesh):
    placed = (
        P(None, "grp", "slab", None),
        P(None, "grp", "slab", None),
        P(),
        P("grp", "slab", None),
        P("grp", "slab", None),
        P(),
    )
    return jax.shard_map(
        per_device,
        mesh=mesh,
        in_specs=placed,
        out_specs=P(None, "grp", "slab", None),
        check_vma=False,
    )
```

time: 82.7 us -> 57.1 us (0.69)
  the two profiles are of different devices: /device:TPU:6 before, /device:TPU:1 now
where the time goes in v1:
time: 57.1 us; the launch traced here: 57 us
  Pallas kernels  55.4 us (97%)
  local copies, waits for them, and re-layouts  1.58 us (3%)
    pallas_call x1, Pallas kernels, per_device(): pl.pallas_call(kernel, out_shape=jax.ShapeDtypeStruct(flat, F32), in_spec...  55.4 us
    unnamed x1, local copies, waits for them, and re-layouts  1.58 us

profile of v1, /device:TPU:1, one launch (start us, length us, event | category | flops | bytes accessed | tf_op | source)
XLA Modules:
  0.0 57.0 jit_solution(9748055523629309283)
XLA Ops:
  0.0 55.4 %shard_map.190 = f32[9,32,128]{2,1,0:T(8,128)} custom-call(f32[9,32,128]{2,1,0:T(8,128)} %bitcast.8, f32[9,32,128]{2,1,0:T(8,128)} %bitcast.9, f32[9,7,9]{2,1,0:T(8,128)} %bitcast.10, s32[32,128]{1,0:T(8,128)} %bitcast.11, s32[32,128]{1,0:T(8,128)} %bitcast.12, s32[32,128]{1,0:T(8,128)} %bitcast.13, bf16[128,384]{1,0:T(8,128)(2,1)} %constant.28.clone.rest_0_, ...), custom_call_target="tpu_custom_call" | custom-call | tf_op jit(solution)/shard_map/pallas_call | solution.py:570
  55.4 1.6 %copy.22 = f32[9,16,2,128]{3,2,1,0:T(2,128)} copy(f32[9,16,2,128]{3,2,1,0:T(2,128)} %bitcast.7) | data formatting | bytes 294912

commit v2 on v1

--- a/solution.py
+++ b/solution.py
@@ -444,19 +444,20 @@
     digit_y, digit_z, digit_x = s // 16, lax.rem(s // 4, 4), lax.rem(s, 4)
 
     def slab_peers(visit):
-        for step_z in (2, 1, 3, 0):
-            base = lax.rem(digit_z + step_z, 4) * 4
+        for steps_z in ((2,), (1, 3), (0,)):
+            bases = [lax.rem(digit_z + step_z, 4) * 4 for step_z in steps_z]
 
             def row(step_y, carry):
-                start = lax.rem(digit_y + step_y, 4) * 16 + base
+                start = lax.rem(digit_y + step_y, 4) * 16
                 for step_x in range(4):
-                    visit(start + lax.rem(digit_x + step_x, 4))
+                    for base in bases:
+                        visit(start + base + lax.rem(digit_x + step_x, 4))
                 return carry
 
-            if step_z == 0:
+            if steps_z == (0,):
                 for step_x in range(1, 4):
-                    visit(digit_y * 16 + base + lax.rem(digit_x + step_x, 4))
-            lax.fori_loop(1 if step_z == 0 else 0, 4, row, 0)
+                    visit(digit_y * 16 + bases[0] + lax.rem(digit_x + step_x, 4))
+            lax.fori_loop(1 if steps_z == (0,) else 0, 4, row, 0)
 
     def grp_peers(visit):
         def one(step, carry):
@@ -569,7 +570,7 @@
     flat = (9, 32, N)
     result = pl.pallas_call(
         kernel,
-        out_shape=jax.ShapeDtypeStruct(flat, F32),
+        out_shape=pltpu.VMEM(flat, F32),
         in_specs=[hbm] * (6 + len(CONSTANTS)),
         out_specs=vmem,
         scratch_shapes=[

time: 57.1 us -> 55.4 us (0.970)
  local copies, waits for them, and re-layouts: 1.58 us -> 0.66 us
  Pallas kernels: 55.4 us -> 54.6 us
    unnamed x1, local copies, waits for them, and re-layouts: 1.58 us -> 0.66 us
    pallas_call x1, Pallas kernels: 55.4 us -> 54.6 us  [per_device(): pl.pallas_call(kernel, out_shape=pltpu.VMEM(flat, F32), in_specs=[hbm] *...]
where the time goes in v2:
time: 55.4 us; the launch traced here: 55.3 us
  Pallas kernels  54.6 us (99%)
  local copies, waits for them, and re-layouts  0.66 us (1%)
    pallas_call x1, Pallas kernels, per_device(): pl.pallas_call(kernel, out_shape=pltpu.VMEM(flat, F32), in_specs=[hbm] *...  54.6 us

profile of v2, /device:TPU:1, one launch (start us, length us, event | category | flops | bytes accessed | tf_op | source)
XLA Modules:
  0.0 55.3 jit_solution(10926783025724488563)
XLA Ops:
  0.0 54.6 %shard_map.190 = f32[9,32,128]{2,1,0:T(8,128)S(1)} custom-call(f32[9,32,128]{2,1,0:T(8,128)} %bitcast.8, f32[9,32,128]{2,1,0:T(8,128)} %bitcast.9, f32[9,7,9]{2,1,0:T(8,128)} %bitcast.10, s32[32,128]{1,0:T(8,128)} %bitcast.11, s32[32,128]{1,0:T(8,128)} %bitcast.12, s32[32,128]{1,0:T(8,128)} %bitcast.13, bf16[128,384]{1,0:T(8,128)(2,1)} %constant.28.clone.rest_0_, ...), custom_call_target="tpu_custom_call" | custom-call | tf_op jit(solution)/shard_map/pallas_call | solution.py:571
  54.6 0.7 %copy.22 = f32[9,16,2,128]{3,2,1,0:T(2,128)} copy(f32[9,16,2,128]{3,2,1,0:T(2,128)S(1)} %bitcast.7) | data formatting | bytes 294912

commit v3 on v2

--- a/solution.py
+++ b/solution.py
@@ -16,6 +16,7 @@
 BF16 = jnp.bfloat16
 ROOT_HALF = float(np.sqrt(0.5))
 MESH = pl.DeviceIdType.MESH
+SLOTS = np.arange(SLAB).reshape(4, 4, 4).transpose(1, 0, 2).reshape(SLAB)
 
 
 def split_const(matrix, axis):
@@ -39,7 +40,7 @@
     forward[0, 1] = (-1.0) ** x
     inverse[1:] = 2.0 * forward[1:]
     inverse[0] = forward[0]
-    return forward.reshape(N, N), inverse.reshape(N, N)
+    return forward[SLOTS].reshape(N, N), inverse[SLOTS].reshape(N, N)
 
 
 def z_tables(first):
@@ -74,7 +75,9 @@
                     inverse[z2, :, 0, h, hi, 1, lo] = -sin
                     inverse[z2, :, 1, h, hi, 0, lo] = sin
                     inverse[z2, :, 1, h, hi, 1, lo] = cos
-    return forward.reshape(256, 384), inverse.reshape(384, 256)
+    forward = forward[..., SLOTS, :].reshape(256, 3, 4, 32).transpose(2, 0, 1, 3).reshape(4, 256, 96)
+    inverse = inverse[:, SLOTS].reshape(3, 4, 32, 256).transpose(1, 0, 2, 3).reshape(4, 96, 256)
+    return forward, inverse
 
 
 def y_outer_tables(corner):
@@ -184,8 +187,8 @@
     return dict(
         wx=split_const(x_forward, 1),
         wxi=split_const(x_inverse, 0),
-        wz=np.stack([split_const(pair[0], 1) for pair in z_pairs]),
-        wzi=np.stack([split_const(pair[1], 1) for pair in z_pairs]),
+        wz=np.stack([split_const(pair[0], 2) for pair in z_pairs]),
+        wzi=np.stack([split_const(pair[1], 2) for pair in z_pairs]),
         wy=np.stack([split_const(pair[0], 1) for pair in y_pairs]),
         wyi=np.stack([split_const(pair[1], 1) for pair in y_pairs]),
         wl=split_const(inner_forward, 0),
@@ -257,9 +260,8 @@
     return dot(thirds(rows.T, 1), wxi, ((1,), (0,)))
 
 
-def z_forward(rows, wz):
-    lane = lanes((N, N))
-    low = lane < 64
+def z_forward_part(rows, wz):
+    low = lanes((32, N)) < 64
     main, rest = rows[:, :N], rows[:, N:]
     parts = jnp.concatenate(
         [
@@ -269,14 +271,18 @@
         ],
         axis=0,
     )
-    both = dot(wz, thirds(parts, 0), ((1,), (0,)))
+    return dot(wz, thirds(parts, 0), ((1,), (0,)))
+
+
+def z_forward_end(both):
+    lane = lanes((N, N))
     first, second = both[:N], both[N:]
     edge = jnp.where(lane < 96, first, jnp.roll(second, 32, axis=1))
     edge = jnp.where((lane % 8 == sublanes((N, N)) % 8) & (lane >= 64), edge, 0.0)
-    return jnp.where(low, first, jnp.roll(second, 64, axis=1)), edge.reshape(16, 8, N).sum(axis=1)
-
-
-def z_inverse(rows, edge, wzi):
+    return jnp.where(lane < 64, first, jnp.roll(second, 64, axis=1)), edge.reshape(16, 8, N).sum(axis=1)
+
+
+def z_inverse_begin(rows, edge):
     lane = lanes((N, N))
     low = lane < 64
     edge = jnp.broadcast_to(edge[:, None, :], (16, 8, N)).reshape(N, N)
@@ -284,8 +290,14 @@
     parts = jnp.concatenate(
         [jnp.where(low, rows, edge), jnp.where(low, jnp.roll(rows, 64, axis=1), jnp.roll(edge, 96, axis=1))], axis=0
     )
-    planes = dot(wzi, thirds(parts, 0), ((1,), (0,)))
-    first, second, third = planes[:N], planes[N : 2 * N], planes[2 * N :]
+    return thirds(parts, 0)
+
+
+def z_inverse_part(parts, wzi):
+    lane = lanes((32, N))
+    low = lane < 64
+    planes = dot(wzi, parts, ((1,), (0,)))
+    first, second, third = planes[:32], planes[32:64], planes[64:]
     main = jnp.where(low, first, jnp.roll(second, 64, axis=1))
     rest = jnp.where(low, third, jnp.where(lane < 96, first, jnp.roll(second, 32, axis=1)))
     return jnp.concatenate([main, rest], axis=1)
@@ -407,8 +419,9 @@
         wx, wxi, wz, wzi, wy, wyi, wl, wli, we, wei, tw, dx, dy, dz,
         fields, right_side, contrast, phase, grain, orientation,
         send1, recv1, send2, recv2, send3, recv3, send4, recv4,
+        edge2_out, edge2_in, edge3_out, edge3_in,
         coef, own_real, own_imag, alpha, beta,
-        load_sems, send_sems, recv_sems,
+        load_sems, send_sems, recv_sems, slab_send, slab_recv,
     ) = rest[len(CONSTANTS):]
     g = lax.axis_index("grp")
     s = lax.axis_index("slab")
@@ -443,21 +456,25 @@
 
     digit_y, digit_z, digit_x = s // 16, lax.rem(s // 4, 4), lax.rem(s, 4)
 
-    def slab_peers(visit):
-        for steps_z in ((2,), (1, 3), (0,)):
-            bases = [lax.rem(digit_z + step_z, 4) * 4 for step_z in steps_z]
-
-            def row(step_y, carry):
-                start = lax.rem(digit_y + step_y, 4) * 16
-                for step_x in range(4):
-                    for base in bases:
-                        visit(start + base + lax.rem(digit_x + step_x, 4))
-                return carry
-
-            if steps_z == (0,):
-                for step_x in range(1, 4):
-                    visit(digit_y * 16 + bases[0] + lax.rem(digit_x + step_x, 4))
-            lax.fori_loop(1 if steps_z == (0,) else 0, 4, row, 0)
+    my_slot = digit_z * 16 + digit_y * 4 + digit_x
+    core = lax.rem(g, 2)
+
+    def slab_peers(visit, steps_z):
+        places = [lax.rem(digit_z + step_z, 4) for step_z in steps_z]
+
+        def row(step_y, carry):
+            y = lax.rem(digit_y + step_y, 4)
+            for step_x in range(4):
+                x = lax.rem(digit_x + step_x, 4)
+                for place in places:
+                    visit(y * 16 + place * 4 + x, place * 16 + y * 4 + x)
+            return carry
+
+        if steps_z == (0,):
+            for step_x in range(1, 4):
+                x = lax.rem(digit_x + step_x, 4)
+                visit(digit_y * 16 + digit_z * 4 + x, digit_z * 16 + digit_y * 4 + x)
+        lax.fori_loop(1 if steps_z == (0,) else 0, 4, row, 0)
 
     def grp_peers(visit):
         def one(step, carry):
@@ -467,43 +484,56 @@
         lax.fori_loop(1, GRP, one, 0)
 
     barrier = pltpu.get_barrier_semaphore()
-    slab_peers(lambda peer: pl.semaphore_signal(barrier, inc=1, device_id={"slab": peer}, device_id_type=MESH))
+    for steps_z in ((2,), (1, 3), (0,)):
+        slab_peers(
+            lambda peer, slot: pl.semaphore_signal(barrier, inc=1, device_id={"slab": peer}, device_id_type=MESH),
+            steps_z,
+        )
     grp_peers(lambda peer: pl.semaphore_signal(barrier, inc=1, device_id={"grp": peer}, device_id_type=MESH))
 
-    def exchange_slab(sent, landed, which):
+    def send_slab(sent, landed, which, steps_z):
+        sem = which * 3 + steps_z[0]
+
+        def start(peer, slot):
+            pltpu.make_async_remote_copy(
+                sent.at[slot], landed.at[my_slot], slab_send.at[sem], slab_recv.at[sem],
+                device_id={"slab": peer}, device_id_type=MESH,
+            ).start()
+
+        slab_peers(start, steps_z)
+
+    def exchange_grp(sent, landed, sem):
         def start(peer):
             pltpu.make_async_remote_copy(
-                sent.at[peer], landed.at[s], send_sems.at[which], recv_sems.at[which],
-                device_id={"slab": peer}, device_id_type=MESH,
-            ).start()
-
-        slab_peers(start)
-        landed[s] = sent[s]
-
-    def exchange_grp(sent, landed, which):
-        def start(peer):
-            pltpu.make_async_remote_copy(
-                sent.at[peer], landed.at[g], send_sems.at[which], recv_sems.at[which],
+                sent.at[peer], landed.at[g], send_sems.at[sem], recv_sems.at[sem],
                 device_id={"grp": peer}, device_id_type=MESH,
             ).start()
 
         grp_peers(start)
         landed[g] = sent[g]
 
-    def arrived(landed, which, count):
-        block = landed.at[pl.ds(0, count)]
-        pltpu.make_async_copy(block, block, recv_sems.at[which]).wait()
-
-    def gone(sent, which, count):
-        block = sent.at[pl.ds(0, count)]
-        pltpu.make_async_copy(block, block, send_sems.at[which]).wait()
+    def finish(buffer, sem, count):
+        block = buffer.at[pl.ds(0, count)]
+        pltpu.make_async_copy(block, block, sem).wait()
 
     loads[0].wait()
     lines = force_lines(lambda part, z2: fields[part, pl.ds(z2, 16, stride=2), :])
     loads[1].wait()
     send1[...] = x_forward(lines, wx[...]).reshape(SLAB, 2, 2 * N)
     pl.semaphore_wait(barrier, SLAB - 1 + GRP - 1)
-    exchange_slab(send1, recv1, 0)
+
+    @pl.when(core == 0)
+    def _():
+        send_slab(send1, recv1, 0, (2,))
+        send_slab(send1, recv1, 0, (1, 3))
+
+    @pl.when(core == 1)
+    def _():
+        send_slab(send1, recv1, 0, (1, 3))
+        send_slab(send1, recv1, 0, (2,))
+
+    send_slab(send1, recv1, 0, (0,))
+    recv1[my_slot] = send1[my_slot]
 
     for load in loads[2:6]:
         load.wait()
@@ -525,30 +555,62 @@
         load.wait()
     own_real[...], own_imag[...], alpha[...], beta[...] = operator_tables(dx, dy, dz)
 
-    arrived(recv1, 0, SLAB - 1)
-    rows, edge = z_forward(recv1[...].reshape(N, 2 * N), wz[...])
-    send2[:, 0:16, :] = rows.reshape(GRP, 16, N)
-    send2[:, 16:18, :] = edge.reshape(GRP, 2, N)
-    exchange_grp(send2, recv2, 1)
-
-    arrived(recv2, 1, GRP - 1)
+    def part1(step_z):
+        place = lax.rem(digit_z + step_z, 4)
+        return z_forward_part(recv1[pl.ds(place * 16, 16)].reshape(32, 2 * N), wz[place])
+
+    finish(recv1, slab_recv.at[0], 15)
+    total = part1(0)
+    finish(recv1, slab_recv.at[1], 32)
+    total = total + part1(1) + part1(3)
+    finish(recv1, slab_recv.at[2], 16)
+    rows, edge = z_forward_end(total + part1(2))
+    send2[...] = rows.reshape(GRP, 16, N)
+    exchange_grp(send2, recv2, 0)
+    edge2_out[...] = edge.reshape(GRP, 2, N)
+    exchange_grp(edge2_out, edge2_in, 1)
+
+    finish(recv2, recv_sems.at[0], GRP - 1)
+    finish(edge2_in, recv_sems.at[1], GRP - 1)
     real, imag = y_forward(
-        recv2[:, 0:16, :].reshape(N, N), recv2[:, 16:18, :].reshape(16, N), corner, wy[...], wl[...], we[...], tw
+        recv2[...].reshape(N, N), edge2_in[...].reshape(16, N), corner, wy[...], wl[...], we[...], tw
     )
     real, imag = operator(real, imag, own_real[...], own_imag[...], alpha[...], beta[...])
     rows, edge_real, edge_imag = y_inverse(real, imag, corner, wyi[...], wli[...], wei[...], tw)
-    send3[:, 0:16, :] = rows.reshape(GRP, 16, N)
-    send3[:, 16:17, :] = edge_real.reshape(GRP, 1, N)
-    send3[:, 17:18, :] = edge_imag.reshape(GRP, 1, N)
+    send3[...] = rows.reshape(GRP, 16, N)
     exchange_grp(send3, recv3, 2)
-
-    arrived(recv3, 2, GRP - 1)
-    send4[...] = z_inverse(
-        recv3[:, 0:16, :].reshape(N, N), recv3[:, 16:18, :].reshape(16, N), wzi[...]
-    ).reshape(SLAB, 2, 2 * N)
-    exchange_slab(send4, recv4, 3)
-
-    arrived(recv4, 3, SLAB - 1)
+    edge3_out[:, 0:1, :] = edge_real.reshape(GRP, 1, N)
+    edge3_out[:, 1:2, :] = edge_imag.reshape(GRP, 1, N)
+    exchange_grp(edge3_out, edge3_in, 3)
+
+    finish(recv3, recv_sems.at[2], GRP - 1)
+    finish(edge3_in, recv_sems.at[3], GRP - 1)
+    parts = z_inverse_begin(recv3[...].reshape(N, N), edge3_in[...].reshape(16, N))
+
+    def part4(step_z):
+        place = lax.rem(digit_z + step_z, 4)
+        send4[pl.ds(place * 16, 16)] = z_inverse_part(parts, wzi[place]).reshape(16, 2, 2 * N)
+
+    part4(2)
+
+    @pl.when(core == 0)
+    def _():
+        send_slab(send4, recv4, 1, (2,))
+
+    part4(1)
+    part4(3)
+    send_slab(send4, recv4, 1, (1, 3))
+
+    @pl.when(core == 1)
+    def _():
+        send_slab(send4, recv4, 1, (2,))
+
+    part4(0)
+    send_slab(send4, recv4, 1, (0,))
+    recv4[my_slot] = send4[my_slot]
+
+    for sem, count in ((3, 15), (4, 32), (5, 16)):
+        finish(recv4, slab_recv.at[sem], count)
     green = gradients(x_inverse(recv4[...].reshape(N, 2 * N), wxi[...]))
     for i in range(9):
         total = jnp.concatenate([right_side[i, pl.ds(z2, 16, stride=2), :] for z2 in range(2)], axis=0)
@@ -557,10 +619,11 @@
         for z2 in range(2):
             out[i, pl.ds(z2, 16, stride=2), :] = total[z2 * 16 : z2 * 16 + 16]
 
-    gone(send1, 0, SLAB - 1)
-    gone(send2, 1, GRP - 1)
-    gone(send3, 2, GRP - 1)
-    gone(send4, 3, SLAB - 1)
+    for which, sent in enumerate((send1, send4)):
+        for sem, count in enumerate((15, 32, 16)):
+            finish(sent, slab_send.at[which * 3 + sem], count)
+    for sem, sent in enumerate((send2, edge2_out, send3, edge3_out)):
+        finish(sent, send_sems.at[sem], GRP - 1)
 
 
 def per_device(adjoint, source, contrast, phase_id, grain_id, orientation):
@@ -576,8 +639,8 @@
         scratch_shapes=[
             pltpu.VMEM((128, 384), BF16),
             pltpu.VMEM((384, 128), BF16),
-            pltpu.VMEM((256, 1152), BF16),
-            pltpu.VMEM((384, 768), BF16),
+            pltpu.VMEM((4, 256, 288), BF16),
+            pltpu.VMEM((4, 96, 768), BF16),
             pltpu.VMEM((144, 384), BF16),
             pltpu.VMEM((128, 432), BF16),
             pltpu.VMEM((1152, 256), BF16),
@@ -596,12 +659,16 @@
             pltpu.VMEM((32, N), jnp.int32),
             pltpu.VMEM((SLAB, 2, 2 * N), F32),
             pltpu.VMEM((SLAB, 2, 2 * N), F32),
-            pltpu.VMEM((GRP, 24, N), F32),
-            pltpu.VMEM((GRP, 24, N), F32),
-            pltpu.VMEM((GRP, 24, N), F32),
-            pltpu.VMEM((GRP, 24, N), F32),
+            pltpu.VMEM((GRP, 16, N), F32),
+            pltpu.VMEM((GRP, 16, N), F32),
+            pltpu.VMEM((GRP, 16, N), F32),
+            pltpu.VMEM((GRP, 16, N), F32),
             pltpu.VMEM((SLAB, 2, 2 * N), F32),
             pltpu.VMEM((SLAB, 2, 2 * N), F32),
+            pltpu.VMEM((GRP, 2, N), F32),
+            pltpu.VMEM((GRP, 2, N), F32),
+            pltpu.VMEM((GRP, 2, N), F32),
+            pltpu.VMEM((GRP, 2, N), F32),
             pltpu.VMEM((81, 32, N), F32),
             pltpu.VMEM((72, N), F32),
             pltpu.VMEM((72, N), F32),
@@ -610,6 +677,8 @@
             pltpu.SemaphoreType.DMA((20,)),
             pltpu.SemaphoreType.DMA((4,)),
             pltpu.SemaphoreType.DMA((4,)),
+            pltpu.SemaphoreType.DMA((6,)),
+            pltpu.SemaphoreType.DMA((6,)),
         ],
         compiler_params=pltpu.CompilerParams(
             collective_id=0, has_side_effects=True, vmem_limit_bytes=60 * 1024 * 1024

time: 55.4 us -> 56.4 us (1.018)
  Pallas kernels: 54.6 us -> 55.7 us
    pallas_call x1, Pallas kernels: 54.6 us -> 55.7 us  [per_device(): pl.pallas_call(kernel, out_shape=pltpu.VMEM(flat, F32), in_specs=[hbm] *...]
where the time goes in v3:
time: 56.4 us; the launch traced here: 56.3 us
  Pallas kernels  55.7 us (99%)
  local copies, waits for them, and re-layouts  0.66 us (1%)
    pallas_call x1, Pallas kernels, per_device(): pl.pallas_call(kernel, out_shape=pltpu.VMEM(flat, F32), in_specs=[hbm] *...  55.7 us

profile of v3, /device:TPU:1, one launch (start us, length us, event | category | flops | bytes accessed | tf_op | source)
XLA Modules:
  0.0 56.3 jit_solution(3437019588920876330)
XLA Ops:
  0.0 55.7 %shard_map.190 = f32[9,32,128]{2,1,0:T(8,128)S(1)} custom-call(f32[9,32,128]{2,1,0:T(8,128)} %bitcast.8, f32[9,32,128]{2,1,0:T(8,128)} %bitcast.9, f32[9,7,9]{2,1,0:T(8,128)} %bitcast.10, s32[32,128]{1,0:T(8,128)} %bitcast.11, s32[32,128]{1,0:T(8,128)} %bitcast.12, s32[32,128]{1,0:T(8,128)} %bitcast.13, bf16[128,384]{1,0:T(8,128)(2,1)} %constant.28.clone.rest_0_, ...), custom_call_target="tpu_custom_call" | custom-call | tf_op jit(solution)/shard_map/pallas_call | solution.py:634
  55.7 0.7 %copy.22 = f32[9,16,2,128]{3,2,1,0:T(2,128)} copy(f32[9,16,2,128]{3,2,1,0:T(2,128)S(1)} %bitcast.7) | data formatting | bytes 294912

commit v4 on v3

--- a/solution.py
+++ b/solution.py
@@ -522,18 +522,7 @@
     send1[...] = x_forward(lines, wx[...]).reshape(SLAB, 2, 2 * N)
     pl.semaphore_wait(barrier, SLAB - 1 + GRP - 1)
 
-    @pl.when(core == 0)
-    def _():
-        send_slab(send1, recv1, 0, (2,))
-        send_slab(send1, recv1, 0, (1, 3))
-
-    @pl.when(core == 1)
-    def _():
-        send_slab(send1, recv1, 0, (1, 3))
-        send_slab(send1, recv1, 0, (2,))
-
-    send_slab(send1, recv1, 0, (0,))
-    recv1[my_slot] = send1[my_slot]
+    send_slab(send1, recv1, 0, (2,))
 
     for load in loads[2:6]:
         load.wait()
@@ -551,6 +540,9 @@
         for t in range(6):
             value = jnp.where(masks[t], contrast[pair // 9, t, pair % 9], value)
         coef[pair] = value
+    send_slab(send1, recv1, 0, (1, 3))
+    send_slab(send1, recv1, 0, (0,))
+    recv1[my_slot] = send1[my_slot]
     for load in loads[6:]:
         load.wait()
     own_real[...], own_imag[...], alpha[...], beta[...] = operator_tables(dx, dy, dz)
@@ -592,19 +584,11 @@
         send4[pl.ds(place * 16, 16)] = z_inverse_part(parts, wzi[place]).reshape(16, 2, 2 * N)
 
     part4(2)
-
-    @pl.when(core == 0)
-    def _():
-        send_slab(send4, recv4, 1, (2,))
-
+    send_slab(send4, recv4, 1, (2,))
     part4(1)
     part4(3)
+    finish(send4, slab_send.at[5], 16)
     send_slab(send4, recv4, 1, (1, 3))
-
-    @pl.when(core == 1)
-    def _():
-        send_slab(send4, recv4, 1, (2,))
-
     part4(0)
     send_slab(send4, recv4, 1, (0,))
     recv4[my_slot] = send4[my_slot]
@@ -620,8 +604,9 @@
             out[i, pl.ds(z2, 16, stride=2), :] = total[z2 * 16 : z2 * 16 + 16]
 
     for which, sent in enumerate((send1, send4)):
-        for sem, count in enumerate((15, 32, 16)):
+        for sem, count in enumerate((15, 32)):
             finish(sent, slab_send.at[which * 3 + sem], count)
+    finish(send1, slab_send.at[2], 16)
     for sem, sent in enumerate((send2, edge2_out, send3, edge3_out)):
         finish(sent, send_sems.at[sem], GRP - 1)
 

time: 56.4 us -> 53.5 us (0.949); the launches traced: 56.3 us -> 52.8 us
  Pallas kernels: 55.7 us -> 52.1 us
    pallas_call x1, Pallas kernels: 55.7 us -> 52.1 us  [per_device(): pl.pallas_call(kernel, out_shape=pltpu.VMEM(flat, F32), in_specs=[hbm] *...]
where the time goes in v4:
time: 53.5 us; the launch traced here: 52.8 us
  Pallas kernels  52.1 us (97%)
  local copies, waits for them, and re-layouts  0.66 us (1%)
    pallas_call x1, Pallas kernels, per_device(): pl.pallas_call(kernel, out_shape=pltpu.VMEM(flat, F32), in_specs=[hbm] *...  52.1 us

profile of v4, /device:TPU:1, one launch (start us, length us, event | category | flops | bytes accessed | tf_op | source)
XLA Modules:
  0.0 52.8 jit_solution(6908810352172355814)
XLA Ops:
  0.0 52.1 %shard_map.190 = f32[9,32,128]{2,1,0:T(8,128)S(1)} custom-call(f32[9,32,128]{2,1,0:T(8,128)} %bitcast.8, f32[9,32,128]{2,1,0:T(8,128)} %bitcast.9, f32[9,7,9]{2,1,0:T(8,128)} %bitcast.10, s32[32,128]{1,0:T(8,128)} %bitcast.11, s32[32,128]{1,0:T(8,128)} %bitcast.12, s32[32,128]{1,0:T(8,128)} %bitcast.13, bf16[128,384]{1,0:T(8,128)(2,1)} %constant.28.clone.rest_0_, ...), custom_call_target="tpu_custom_call" | custom-call | tf_op jit(solution)/shard_map/pallas_call | solution.py:619
  52.1 0.7 %copy.22 = f32[9,16,2,128]{3,2,1,0:T(2,128)} copy(f32[9,16,2,128]{3,2,1,0:T(2,128)S(1)} %bitcast.7) | data formatting | bytes 294912

commit v5 on v4

--- a/solution.py
+++ b/solution.py
@@ -463,8 +463,8 @@
         places = [lax.rem(digit_z + step_z, 4) for step_z in steps_z]
 
         def row(step_y, carry):
-            y = lax.rem(digit_y + step_y, 4)
-            for step_x in range(4):
+            y = lax.rem(digit_y + (step_y + 2 if steps_z != (0,) else step_y), 4)
+            for step_x in (2, 1, 3, 0):
                 x = lax.rem(digit_x + step_x, 4)
                 for place in places:
                     visit(y * 16 + place * 4 + x, place * 16 + y * 4 + x)
@@ -534,13 +534,22 @@
         entry = jnp.where(high == row, jnp.take_along_axis(line, low, axis=1), entry)
     ceramic = jnp.concatenate([phase[pl.ds(z2, 16, stride=2), :] for z2 in range(2)], axis=0) == 1
     entry = jnp.where(ceramic, entry, 6)
+
+    @pl.when(core == 0)
+    def _():
+        send_slab(send1, recv1, 0, (1, 3))
+
     masks = [entry == t for t in range(6)]
     for pair in range(81):
         value = jnp.full((32, N), contrast[pair // 9, 6, pair % 9], F32)
         for t in range(6):
             value = jnp.where(masks[t], contrast[pair // 9, t, pair % 9], value)
         coef[pair] = value
-    send_slab(send1, recv1, 0, (1, 3))
+
+    @pl.when(core == 1)
+    def _():
+        send_slab(send1, recv1, 0, (1, 3))
+
     send_slab(send1, recv1, 0, (0,))
     recv1[my_slot] = send1[my_slot]
     for load in loads[6:]:

time: 53.5 us -> 52.2 us (0.976)
  Pallas kernels: 52.1 us -> 50.9 us
    pallas_call x1, Pallas kernels: 52.1 us -> 50.9 us  [per_device(): pl.pallas_call(kernel, out_shape=pltpu.VMEM(flat, F32), in_specs=[hbm] *...]
where the time goes in v5:
time: 52.2 us; the launch traced here: 51.6 us
  Pallas kernels  50.9 us (98%)
  local copies, waits for them, and re-layouts  0.66 us (1%)
    pallas_call x1, Pallas kernels, per_device(): pl.pallas_call(kernel, out_shape=pltpu.VMEM(flat, F32), in_specs=[hbm] *...  50.9 us

profile of v5, /device:TPU:1, one launch (start us, length us, event | category | flops | bytes accessed | tf_op | source)
XLA Modules:
  0.0 51.6 jit_solution(13617346818263331213)
XLA Ops:
  0.0 50.9 %shard_map.190 = f32[9,32,128]{2,1,0:T(8,128)S(1)} custom-call(f32[9,32,128]{2,1,0:T(8,128)} %bitcast.8, f32[9,32,128]{2,1,0:T(8,128)} %bitcast.9, f32[9,7,9]{2,1,0:T(8,128)} %bitcast.10, s32[32,128]{1,0:T(8,128)} %bitcast.11, s32[32,128]{1,0:T(8,128)} %bitcast.12, s32[32,128]{1,0:T(8,128)} %bitcast.13, bf16[128,384]{1,0:T(8,128)(2,1)} %constant.28.clone.rest_0_, ...), custom_call_target="tpu_custom_call" | custom-call | tf_op jit(solution)/shard_map/pallas_call | solution.py:628
  50.9 0.7 %copy.22 = f32[9,16,2,128]{3,2,1,0:T(2,128)} copy(f32[9,16,2,128]{3,2,1,0:T(2,128)S(1)} %bitcast.7) | data formatting | bytes 294912

commit v6 on v5

--- a/solution.py
+++ b/solution.py
@@ -562,10 +562,10 @@
 
     finish(recv1, slab_recv.at[0], 15)
     total = part1(0)
+    finish(recv1, slab_recv.at[2], 16)
+    total = total + part1(2)
     finish(recv1, slab_recv.at[1], 32)
-    total = total + part1(1) + part1(3)
-    finish(recv1, slab_recv.at[2], 16)
-    rows, edge = z_forward_end(total + part1(2))
+    rows, edge = z_forward_end(total + part1(1) + part1(3))
     send2[...] = rows.reshape(GRP, 16, N)
     exchange_grp(send2, recv2, 0)
     edge2_out[...] = edge.reshape(GRP, 2, N)

time: 52.2 us -> 53.3 us (1.021)
  the two profiles are of different devices: /device:TPU:1 before, /device:TPU:8 now
where the time goes in v6:
time: 53.3 us; the launch traced here: 53.2 us
  Pallas kernels  52.5 us (98%)
  local copies, waits for them, and re-layouts  0.66 us (1%)
    pallas_call x1, Pallas kernels, per_device(): pl.pallas_call(kernel, out_shape=pltpu.VMEM(flat, F32), in_specs=[hbm] *...  52.5 us

profile of v6, /device:TPU:8, one launch (start us, length us, event | category | flops | bytes accessed | tf_op | source)
XLA Modules:
  0.0 53.2 jit_solution(307972322245281324)
XLA Ops:
  0.0 52.5 %shard_map.190 = f32[9,32,128]{2,1,0:T(8,128)S(1)} custom-call(f32[9,32,128]{2,1,0:T(8,128)} %bitcast.8, f32[9,32,128]{2,1,0:T(8,128)} %bitcast.9, f32[9,7,9]{2,1,0:T(8,128)} %bitcast.10, s32[32,128]{1,0:T(8,128)} %bitcast.11, s32[32,128]{1,0:T(8,128)} %bitcast.12, s32[32,128]{1,0:T(8,128)} %bitcast.13, bf16[128,384]{1,0:T(8,128)(2,1)} %constant.28.clone.rest_0_, ...), custom_call_target="tpu_custom_call" | custom-call | tf_op jit(solution)/shard_map/pallas_call | solution.py:628
  52.5 0.7 %copy.22 = f32[9,16,2,128]{3,2,1,0:T(2,128)} copy(f32[9,16,2,128]{3,2,1,0:T(2,128)S(1)} %bitcast.7) | data formatting | bytes 294912
